TPU v7x, 128 devices: a whole 4x4x4 slice. The times are simulated.
128 devices in a mesh: occ: 8 (over y_hi, x), vir: 16 (over z, y_lo, core).
Axes of the slice: x: 4, y: 4 (y_hi: 2, y_lo: 2; y = y_hi * 2 + y_lo), z: 4, core: 2. Of those that a mesh axis runs over, the one named last changes fastest.
Arguments:
- amplitudes: float32 [4, 32, 128, 128], P(None, 'occ', 'vir'), may hold values from -6 to 6
- vv_factors: float32 [768, 128, 128], P('occ', 'vir'), may hold values from -0.3 to 0.3
- ov_factors: float32 [768, 32, 128], P(None, 'occ', 'vir'), may hold values from -0.3 to 0.3
- occ_irreps: int32 [32], replicated, may hold values from 0 to 7
- vir_irreps: int32 [128], replicated, may hold values from 0 to 7
- aux_irreps: int32 [768], replicated, may hold values from 0 to 7
Outputs:
- residual: float32 [4, 32, 128, 128], P(None, 'occ', 'vir')
Inputs may be any that keep to these rules, and one draw needn't show every extreme that they name: `vir_irreps`: irrep labels of the point group D2h.
All inputs are finite; a program needn't handle non-finite values.
Results may differ from a plain program's by a relative error of at most 0.000086.
Values sent between devices are 32-bit elements; how exact they have to be, the bound alone decides.
No kernel may reach another device: no remote copies, remote signals or barrier semaphores. Data moves between devices by JAX's collectives and lax.ppermute only.
A program may use at most 192 MiB of HBM per device.

v0:
```python
import jax
import jax.numpy as jnp
from jax import lax
from jax.sharding import PartitionSpec as P


def allowed(left, right, target):
    return (jnp.bitwise_xor(left, right) == target).astype(jnp.float32)


def shards(amplitudes, vv_factors, ov_factors, occ_irreps, vir_irreps, aux_irreps):
    high = lax.Precision.HIGHEST
    aux_local = vv_factors.shape[0]
    vir_local = vv_factors.shape[1]
    occ_local = amplitudes.shape[1]
    occ_index = lax.axis_index("occ")
    vir_index = lax.axis_index("vir")
    aux_mine = lax.dynamic_slice_in_dim(aux_irreps, occ_index * aux_local, aux_local)
    vir_mine = lax.dynamic_slice_in_dim(vir_irreps, vir_index * vir_local, vir_local)
    occ_mine = lax.dynamic_slice_in_dim(occ_irreps, occ_index * occ_local, occ_local)
    vv_local = vv_factors * allowed(
        vir_mine[None, :, None], vir_irreps[None, None, :], aux_mine[:, None, None]
    )
    vv_wide = lax.all_gather(vv_factors, "vir", axis=1, tiled=True)
    vv_wide = vv_wide * allowed(
        vir_irreps[None, :, None], vir_irreps[None, None, :], aux_mine[:, None, None]
    )
    pair_all = lax.all_gather(amplitudes, "occ", axis=1, tiled=True)
    inter = jnp.einsum("qac,qbd->acbd", vv_local, vv_wide, precision=high)
    partial_sum = jnp.einsum(
        "ijcd,acbd->ijab",
        lax.all_gather(pair_all, "vir", axis=2, tiled=True),
        inter,
        precision=high,
    )
    ladder = lax.psum_scatter(partial_sum, "occ", scatter_dimension=1, tiled=True)
    swapped = lax.all_to_all(amplitudes, "vir", split_axis=3, concat_axis=2, tiled=True)
    cycle_amps = 2.0 * amplitudes - jnp.transpose(swapped, (0, 1, 3, 2))
    ov_wide = lax.all_gather(ov_factors, "vir", axis=2, tiled=True)
    ov_wide = ov_wide * allowed(
        occ_mine[None, :, None], vir_irreps[None, None, :], aux_irreps[:, None, None]
    )
    factor_part = jnp.einsum("ikac,qkc->iaq", cycle_amps, ov_wide, precision=high)
    factor = lax.psum(factor_part, "occ")
    cycle = jnp.einsum("iaq,qjb->ijab", factor, ov_wide, precision=high)
    return ladder + cycle


def solution(mesh):
    placed = (
        P(None, "occ", "vir", None),
        P("occ", "vir", None),
        P(None, "occ", "vir"),
        P(),
        P(),
        P(),
    )
    return jax.shard_map(
        shards, mesh=mesh, in_specs=placed, out_specs=P(None, "occ", "vir", None), check_vma=False
    )
```

profile of v0, /device:TPU:1, one launch (start us, length us, event | category | flops | bytes accessed | tf_op | source)
XLA Modules:
  0.0 341.8 jit_solution(5576453759396806326)
XLA Ops:
  6.5 0.7 all-gather.8.cloned.1.call-update
  8.1 0.8 copy.19
  8.9 30.4 %all_gather.13 = f32[4,32,8,128]{3,2,0,1:T(8,128)S(1)} all-gather(f32[4,4,8,128]{3,2,0,1:T(8,128)S(1)} %copy.19), channel_id=1, replica_groups=mesh['occ'=8,'vir'=16] {'occ'}, dimensions={1}, use_global_device_ids=true | all-gather | bytes 589824 | tf_op jit(solution)/shard_map/all_gather | solution.py:28
  39.3 1.1 copy.20
  40.4 1.4 copy.23
  41.9 1.8 reshape.105
  43.6 12.5 %all-to-all-start = ((f32[16,1,1024]{2,1,0:T(1,128)}), f32[16,1,1024]{2,1,0:T(1,128)S(1)}, u32[]{:S(2)}, u32[]{:S(2)}) async-start(f32[16,1,1024]{2,1,0:T(1,128)} %reshape.105), calls=%async_computation.1 | async-start | bytes 131072 | tf_op jit(solution)/shard_map/all_to_all | solution.py:37
  56.2 0.8 dynamic_slice.10
  57.0 0.7 dynamic_slice.9
  57.7 0.7 dynamic_slice.11
  58.4 0.7 broadcast_xor_fusion.1
  59.2 0.8 broadcast_xor_fusion
  60.0 1.2 select_bitcast_fusion
  61.2 0.7 broadcast_xor_fusion.2
  62.9 0.8 reduce
  63.7 1.2 reshape.106
  66.1 3.2 fusion.14
  69.6 32.1 %all-gather.4.cloned.1.call-done = f32[96,128,128]{2,1,0:T(8,128)} async-done(((f32[96,8,128]{2,1,0:T(8,128)}), f32[96,128,128]{2,1,0:T(8,128)}) %all-gather.4.cloned.1.call-update) | async-done | bytes 6291472 | tf_op jit(solution)/shard_map/all_gather | solution.py:24
  101.7 3.3 compare_select_fusion
  105.0 59.2 %convolution_bitcast_fusion = f32[8,128,128,128,1]{3,1,2,0,4:T(8,128)} fusion(f32[96,128,128]{2,1,0:T(8,128)S(1)} %compare_select_fusion, f32[96,8,128,1]{2,1,0,3:T(8,128)S(1)} %select_bitcast_fusion), kind=kOutput, calls=%fused_computation.2 | convolution fusion | flops 19327352832 | bytes 73793536 | tf_op jit(solution)/shard_map/qac,qbd->acbd/dot_general | solution.py:29
  164.2 98.1 %fusion.9 = f32[4,32,8,128]{3,1,0,2:T(8,128)S(1)} fusion(f32[4,32,128,128]{3,1,2,0:T(8,128)} %all-gather.6.cloned.1.call-done, f32[8,128,128,128,1]{3,1,2,0,4:T(8,128)} %convolution_bitcast_fusion), kind=kOutput, calls=%fused_computation.12 | convolution fusion | flops 25769803776 | bytes 76021760 | tf_op jit(solution)/shard_map/ijcd,acbd->ijab/dot_general | solution.py:30
  262.4 1.1 copy.22
  263.5 68.5 %reduce-scatter.2.cloned.1.call-done = f32[4,4,8,128]{3,2,0,1:T(8,128)} async-done(((f32[4,32,8,128]{3,2,0,1:T(8,128)}), f32[4,4,8,128]{3,2,0,1:T(8,128)}) %reduce-scatter.2.cloned.1.call-update) | async-done | bytes 65552 | tf_op jit(solution)/shard_map/reduce_scatter | solution.py:36
  332.0 2.6 fusion.20
  (23 shorter events, 3.9 us)
Async XLA Ops:
  6.5 59.6 %copy-start.1 = (f32[4,4,8,128]{3,2,1,0:T(8,128)S(1)}, f32[4,4,8,128]{3,2,1,0:T(8,128)}, u32[]{:S(2)}) copy-start(f32[4,4,8,128]{3,2,1,0:T(8,128)} %param.6) | copy-start | bytes 196612
  6.5 59.6 %copy-start.2 = (s32[768]{0:T(1024)S(1)}, s32[768]{0:T(1024)}, u32[]{:S(2)}) copy-start(s32[768]{0:T(1024)} %param.11) | copy-start | bytes 9220
  6.5 59.6 %all-gather.8.cloned.1.call-start = ((), (), s32[]{:S(2)}) async-start(), calls=%async_computation.5 | async-start | bytes 1671168 | tf_op jit(solution)/shard_map/all_gather | solution.py:39
  7.3 94.5 %all-gather.4.cloned.1.call-start = ((), (), s32[]{:S(2)}) async-start(), calls=%async_computation.2 | async-start | bytes 6684672 | tf_op jit(solution)/shard_map/all_gather | solution.py:24
  8.0 156.2 %all-gather.6.cloned.1.call-start = ((), (), s32[]{:S(2)}) async-start(), calls=%async_computation.3 | async-start | bytes 8912896 | tf_op jit(solution)/shard_map/all_gather | solution.py:32
  43.6 18.8 %all-to-all-start = ((f32[16,1,1024]{2,1,0:T(1,128)}), f32[16,1,1024]{2,1,0:T(1,128)S(1)}, u32[]{:S(2)}, u32[]{:S(2)}) async-start(f32[16,1,1024]{2,1,0:T(1,128)} %reshape.105), calls=%async_computation.1 | async-start | bytes 131072 | tf_op jit(solution)/shard_map/all_to_all | solution.py:37
  56.2 207.3 %all-reduce.2.cloned.1.call-start = ((), (), s32[]{:S(2)}) async-start(), calls=%async_computation.6 | async-start | bytes 196608 | tf_op jit(solution)/shard_map/psum | solution.py:44
  69.4 262.6 %reduce-scatter.2.cloned.1.call-start = ((), (), s32[]{:S(2)}) async-start(), calls=%async_computation.4 | async-start | bytes 589824 | tf_op jit(solution)/shard_map/reduce_scatter | solution.py:36
  164.2 167.8 %copy-start = (f32[768,4,128]{0,2,1:T(8,128)S(1)}, f32[768,4,128]{0,2,1:T(8,128)}, u32[]{:S(2)}) copy-start(f32[768,4,128]{0,2,1:T(8,128)} %all-gather.8.cloned.1.call-done) | copy-start | bytes 4718596
Sparse Core Ops, SparseCore 0:
  9.0 37.3 all-gather.7
  48.0 53.6 all-gather.3
  103.4 52.1 all-gather.5
  157.9 76.2 all-reduce.1
  263.6 68.3 reduce-scatter.1
where the time goes:
time: 343 us; the launch traced here: 342 us
  matrix products  163 us (48%)
  waiting for transfers between devices  103 us (30%)
  blocking collectives  30.4 us (9%)
  between operations  13.3 us (4%)
  starting transfers between devices  12.8 us (4%)
  local copies, waits for them, and re-layouts  12 us (3%)
  other arithmetic  7.51 us (2%)
    dot_general x1, matrix products, shards(): jnp.einsum('ijcd,acbd->ijab', lax.all_gather(pair_all, 'vir', axis=2, til...  98.1 us
    reduce_scatter x1, waiting for transfers between devices, shards(): lax.psum_scatter(partial_sum, 'occ', scatter_dimension=1, tiled=True)  68.5 us
    dot_general x1, matrix products, shards(): inter = jnp.einsum('qac,qbd->acbd', vv_local, vv_wide, precision=high)  59.2 us
    all_gather x1, waiting for transfers between devices, shards(): vv_wide = lax.all_gather(vv_factors, 'vir', axis=1, tiled=True)  32.1 us
    all_gather x1, blocking collectives, shards(): pair_all = lax.all_gather(amplitudes, 'occ', axis=1, tiled=True)  30.4 us
    all_to_all x1, starting transfers between devices, shards(): lax.all_to_all(amplitudes, 'vir', split_axis=3, concat_axis=2, tiled=True)  12.5 us
  transfers between devices with their start and end apart: 6, of which 3 were waited for; matrix products, arithmetic and copies ran while one was open for 52% of the time, Pallas kernels for 0%

commit v1 on v0

v1 whole, which is shorter than its diff:
```python
import functools

import jax
import jax.numpy as jnp
from jax import lax
from jax.experimental import pallas as pl
from jax.experimental.pallas import tpu as pltpu
from jax.sharding import Mesh, PartitionSpec as P

OCC = ("yh", "x")
ZY = ("z", "yl")
VIR = ("z", "yl", "core")
F32 = jnp.float32
BF16 = jnp.bfloat16
HIGHEST = lax.Precision.HIGHEST
SL = 24
SG = 128
NG = 8
VMEM = pl.BlockSpec(memory_space=pltpu.VMEM)
SMEM = pl.BlockSpec(memory_space=pltpu.SMEM)
LIMIT = 56 * 2**20


def occ_at():
    return lax.axis_index("yh") * 4 + lax.axis_index("x")


def vir_at():
    return lax.axis_index("z") * 4 + lax.axis_index("yl") * 2 + lax.axis_index("core")


def iota(shape, dim):
    return lax.broadcasted_iota(jnp.int32, shape, dim)


def split(x):
    hi = x.astype(BF16)
    return hi, (x - hi.astype(F32)).astype(BF16)


def dot(x, y):
    return jnp.dot(x, y, preferred_element_type=F32)


def dot_t(x, y, precision=None):
    return lax.dot_general(x, y, (((1,), (1,)), ((), ())), precision=precision, preferred_element_type=F32)


def call(body, outs, n_smem, n_vmem, scratch=(), cost=(0, 0)):
    return pl.pallas_call(
        body,
        out_shape=outs,
        in_specs=[SMEM] * n_smem + [VMEM] * n_vmem,
        out_specs=jax.tree.map(lambda _: VMEM, outs),
        scratch_shapes=list(scratch),
        compiler_params=pltpu.CompilerParams(vmem_limit_bytes=LIMIT),
        cost_estimate=pl.CostEstimate(flops=cost[0], bytes_accessed=cost[1], transcendentals=0),
    )


def fold_local(vir_s, lab_ref, b_ref, t_ref, out_ref, roll_ref):
    o, v = occ_at(), vir_at()
    q_lane = jnp.broadcast_to(lab_ref[pl.ds(o, 1), :], (128, 128))
    q_sub = jnp.transpose(q_lane)
    same = (q_sub == q_lane) & (iota((128, 128), 0) < iota((128, 128), 1))
    rank = jnp.sum(same.astype(F32), axis=0, keepdims=True)
    pick = (rank == iota((SL, 128), 0).astype(F32)).astype(F32)[:, :96].astype(BF16)
    y_row = lab_ref[8:9, :]
    for x in range(8):
        keep = (y_row ^ vir_s[v * 8 + x]) == q_sub[:96]
        hi, lo = split(jnp.where(keep, b_ref[:, x, :], 0.0))
        folded = dot(pick, hi) + dot(pick, lo)
        for peer in range(8):
            out_ref[peer, x * SL : (x + 1) * SL, :] = folded
    amps = t_ref[...].reshape(16, 8, 128)
    for k in range(8):
        roll_ref[k] = pltpu.roll(amps, 16 * k, 2) if k else amps
    group = iota((16, 128), 1) // 16
    for peer in range(8):
        block = jnp.zeros((16, 128), F32)
        for c in range(8):
            block = jnp.where(group == c, roll_ref[(c - peer) % 8, :, c, :], block)
        out_ref[peer, 8 * SL : 8 * SL + 16, :] = block


def fold_ov(vir_s, occ_s, aux_ref, c_ref, t_ref, ch_ref, sw_ref):
    o, v = occ_at(), vir_at()
    aux = aux_ref[...]
    member = (aux == iota((NG, 768), 0)).astype(F32)
    before = (iota((768, 768), 0) < iota((768, 768), 1)).astype(F32).astype(BF16)
    rank = jnp.sum(member * dot(member.astype(BF16), before), axis=0, keepdims=True)
    pick = (rank == iota((SG, 768), 0).astype(F32)).astype(F32).astype(BF16)
    c_label = jnp.zeros((8, 1), jnp.int32)
    for c in range(8):
        c_label = jnp.where(iota((8, 1), 0) == c, vir_s[v * 8 + c], c_label)
    for k in range(4):
        keep = (c_label ^ occ_s[o * 4 + k]) == aux
        hi, lo = split(jnp.where(keep, c_ref[k], 0.0))
        ch_ref[8 * k : 8 * k + 8, :] = dot_t(hi, pick) + dot_t(lo, pick)
    sw_ref[...] = jnp.transpose(t_ref[...].reshape(128, 128))


def place(lab_ref, place_ref):
    lane = iota((SL, 128), 1).astype(F32) - iota((SL, 128), 0).astype(F32)
    aux = lab_ref[0:8, :]
    for g in range(NG):
        count = jnp.sum((aux == g).astype(F32), axis=1, keepdims=True)
        start = jnp.zeros((1, 1), F32)
        for block in range(8):
            row = g * 256 + block * SL
            place_ref[row : row + SL, :] = (lane == start).astype(F32)
            start = start + count[block : block + 1, :]
        place_ref[g * 256 + 8 * SL : (g + 1) * 256, :] = jnp.zeros((256 - 8 * SL, 128), F32)


def refold_own(vir_s, lab_ref, r1_ref, ch_ref, sw_ref, out_ref, place_ref, row_ref):
    o, v = occ_at(), vir_at()
    place(lab_ref, place_ref)
    group = iota((1, 128), 1) // 16
    y_row = jnp.broadcast_to(lab_ref[8:9, :], (8, 128))
    mine = jnp.zeros((8 * SL, 128), F32)
    label = jnp.zeros((8, 128), jnp.int32)
    for x in range(8):
        shift = lax.rem(16 * x + 128 - 16 * o, 128)
        block = jnp.concatenate([r1_ref[p, x * SL : (x + 1) * SL, :] for p in range(8)], axis=0)
        mine = jnp.where(group == x, pltpu.roll(block, shift, 1), mine)
        label = jnp.where(group == x, pltpu.roll(y_row, shift, 1) ^ vir_s[v * 8 + x], label)
    mine = jnp.transpose(jnp.concatenate([mine, jnp.zeros((256 - 8 * SL, 128), F32)], axis=0))
    label = jnp.transpose(jnp.broadcast_to(label[0:1], (128, 128)))
    label = jnp.concatenate([label, label], axis=1)
    hi, lo = split(mine)
    hi, lo = hi.astype(F32), lo.astype(F32)
    total = jnp.zeros((256, 128), F32)
    for g in range(NG):
        both = jnp.concatenate([jnp.where(label == g, hi, 0.0), jnp.where(label == g, lo, 0.0)], axis=0)
        total = total + dot(both.astype(BF16), place_ref[g * 256 : (g + 1) * 256, :].astype(BF16))
    row_ref[0] = total[:128] + total[128:]
    row_ref[1] = jnp.transpose(
        jnp.concatenate([r1_ref[p, 8 * SL : 8 * SL + 16, :] for p in range(8)], axis=0)
    )
    for d in range(16):
        own = row_ref[0, pl.ds(d, 8, stride=16), :]
        amps = row_ref[1, pl.ds(d, 8, stride=16), :]
        for peer in range(8):
            out_ref[peer, d * 8 : d * 8 + 8, :] = own
            out_ref[peer, 128 + d * 8 : 136 + d * 8, :] = amps
    for peer in range(8):
        out_ref[peer, 256:288, :] = ch_ref[...]
        out_ref[peer, 288:304, :] = sw_ref[16 * peer : 16 * peer + 16, :]


def refold_rows(vir_s, lab_ref, r1_ref, out_ref, place_ref):
    v = vir_at()
    place(lab_ref, place_ref)
    spread = jnp.concatenate(
        [jnp.transpose(place_ref[128 * n : 128 * n + 128, :]).astype(BF16) for n in range(2 * NG)], axis=1
    )
    y_row = lab_ref[8:9, :]
    pad = jnp.zeros((256 - 8 * SL, 128), F32)
    for x in range(8):
        label = y_row ^ vir_s[v * 8 + x]
        block = jnp.concatenate([r1_ref[p, x * SL : (x + 1) * SL, :] for p in range(8)] + [pad], axis=0)
        hi, lo = split(block)
        both = jnp.concatenate([hi, lo], axis=1)
        total = jnp.zeros((SG, 256), F32)
        for g in range(NG):
            keep = (label == g).astype(F32)
            keep = jnp.concatenate([keep, keep], axis=1).astype(BF16)
            total = total + dot(spread[:, g * 256 : (g + 1) * 256], both * keep)
        hi, lo = split(total[:, :128] + total[:, 128:])
        out_ref[0:128, x * 128 : x * 128 + 128] = hi
        out_ref[128:256, x * 128 : x * 128 + 128] = lo
        out_ref[256:384, x * 128 : x * 128 + 128] = hi


def cycle_first(occ_s, lab_ref, r2_ref, o2_ref, t_ref, y_ref, chat_ref, got_ref):
    o, core = occ_at(), lax.axis_index("core")
    for p in range(8):
        got_ref[2 * p + core] = r2_ref[p, 256:304, :]
        got_ref[2 * p + 1 - core] = o2_ref[p, 256:304, :]
    for k in range(4):
        for n in range(16):
            chat_ref[k * 128 + n * 8 : k * 128 + n * 8 + 8, :] = got_ref[n, 8 * k : 8 * k + 8, :]
    group = iota((8, 128), 1) // 8
    blocks = [got_ref[n, pl.ds(pl.multiple_of(32 + 8 * core, 8), 8), :] for n in range(16)]
    u = []
    for i in range(4):
        row = []
        for k in range(4):
            swapped = jnp.zeros((8, 128), F32)
            for n in range(16):
                shift = (8 * (n - 4 * i - k)) % 128
                swapped = jnp.where(group == n, pltpu.roll(blocks[n], shift, 1) if shift else blocks[n], swapped)
            row.append(2.0 * t_ref[i, k] - swapped)
        u.append(jnp.concatenate(row, axis=1))
    u = jnp.concatenate(u, axis=0)
    label = jnp.concatenate([lab_ref[8:9, :] ^ occ_s[o * 4 + k] for k in range(4)], axis=1)
    rows = jnp.concatenate([jnp.where(label == g, u, 0.0) for g in range(NG)], axis=0)
    y = jnp.dot(rows, chat_ref[...], precision=HIGHEST, preferred_element_type=F32)
    for peer in range(8):
        y_ref[peer] = y


def ladder(vir_s, lab_ref, b1_ref, r2_ref, o2_ref, out_ref, f_ref, t_ref, hi_ref, lo_ref, acc_ref):
    o, v, core = occ_at(), vir_at(), lax.axis_index("core")
    for ref, part in ((r2_ref, core), (o2_ref, 1 - core)):
        for p in range(8):
            f_ref[:, 2 * p + part] = ref[p, 0:128, :].reshape(16, 8, 128)
            t_ref[:, 2 * p + part] = ref[p, 128:256, :].reshape(16, 8, 128)
    acc_ref[...] = jnp.zeros_like(acc_ref)
    c_lane = jnp.broadcast_to(lab_ref[8:9, :], (128, 128))
    bc = jnp.transpose(c_lane) ^ c_lane

    def step(n, carry):
        amps = []
        for half in range(2):
            d = 2 * n + half
            hi, lo = split(f_ref[d].reshape(128, 128))
            w = dot(jnp.concatenate([hi, hi, lo], axis=1), b1_ref[...])
            d_label = vir_s[o * 16 + d]
            for a in range(8):
                keep = bc == (vir_s[v * 8 + a] ^ d_label)
                hi, lo = split(jnp.where(keep, w[:, a * 128 : a * 128 + 128], 0.0))
                hi_ref[a * 128 : a * 128 + 128, half * 128 : half * 128 + 128] = hi
                lo_ref[a * 128 : a * 128 + 128, half * 128 : half * 128 + 128] = lo
            amps.append(t_ref[d].reshape(128, 128))
        hi, lo = split(jnp.concatenate(amps, axis=0))
        r = dot(hi_ref[...], jnp.concatenate([hi, lo], axis=1))
        acc_ref[...] += r[:, :128] + r[:, 128:] + dot(lo_ref[...], hi)
        return carry

    lax.fori_loop(0, 8, step, 0)
    for a in range(8):
        rows = jnp.transpose(acc_ref[a * 128 : a * 128 + 128, :])
        for p in range(8):
            out_ref[p, a] = rows[16 * p : 16 * p + 16, :]


def finish(occ_s, lab_ref, r3_ref, y_ref, chat_ref, out_ref, sum_ref):
    o = occ_at()
    total = r3_ref[0]
    y = y_ref[0]
    for p in range(1, 8):
        total = total + r3_ref[p]
        y = y + y_ref[p]
    sum_ref[...] = total
    z = dot_t(y, chat_ref[...], HIGHEST)
    for j in range(4):
        label = lab_ref[8:9, :] ^ occ_s[o * 4 + j]
        part = jnp.zeros((32, 128), F32)
        for g in range(NG):
            part = jnp.where(label == g, z[g * 32 : g * 32 + 32, j * 128 : j * 128 + 128], part)
        for i in range(4):
            out_ref[i, j] = sum_ref[:, i * 4 + j, :] + part[8 * i : 8 * i + 8, :]


def swap(x, axes):
    return lax.all_to_all(x, axes, 0, 0, tiled=True)


def folded(t, b, c, occ, vir, aux):
    aux8 = jnp.pad(aux.reshape(8, 96), ((0, 0), (0, 32)), constant_values=NG)
    rest = jnp.stack([vir, jnp.pad(occ, (0, 96), constant_values=NG)])
    lab = jnp.concatenate([aux8, rest, jnp.zeros((6, 128), jnp.int32)], axis=0)
    shape = jax.ShapeDtypeStruct
    p1 = call(
        fold_local, shape((8, 8 * SL + 16, 128), F32), 1, 3, [pltpu.VMEM((8, 16, 8, 128), F32)],
        (2 * 2 * 24 * 96 * 1024, 1300000),
    )(vir, lab, b, t)
    r1 = swap(p1, OCC)
    ch, sw = call(
        fold_ov, (shape((32, 128), F32), shape((128, 128), F32)), 2, 3, (), (2 * 8 * 768 * 768 + 4 * 32 * 768 * 128, 300000)
    )(vir, occ, aux.reshape(1, 768), jnp.transpose(c, (1, 2, 0)), t)
    p2 = call(
        refold_own, shape((8, 304, 128), F32), 1, 4, [pltpu.VMEM((2048, 128), F32), pltpu.VMEM((2, 128, 128), F32)],
        (2 * 256 * 2048 * 128, 2300000),
    )(vir, lab, r1, ch, sw)
    r2 = swap(p2, ZY)
    b1 = call(
        refold_rows, shape((384, 1024), BF16), 1, 2, [pltpu.VMEM((2048, 128), F32)], (2 * 128 * 2048 * 2048, 1700000)
    )(vir, lab, r1)
    o2 = lax.ppermute(r2, "core", [(0, 1), (1, 0)])
    yp, chat = call(
        cycle_first, (shape((8, 256, 128), F32), shape((512, 128), F32)), 1, 4, [pltpu.VMEM((16, 48, 128), F32)],
        (6 * 2 * 256 * 512 * 128, 4000000),
    )(occ, lab, r2, o2, t)
    yr = swap(yp, OCC)
    p3 = call(
        ladder, shape((8, 8, 16, 128), F32), 1, 4,
        [
            pltpu.VMEM((16, 16, 8, 128), F32),
            pltpu.VMEM((16, 16, 8, 128), F32),
            pltpu.VMEM((1024, 256), BF16),
            pltpu.VMEM((1024, 256), BF16),
            pltpu.VMEM((1024, 128), F32),
        ],
        (6 * 2048 * 1024 * 256, 4000000),
    )(vir, lab, b1, r2, o2)
    r3 = swap(p3, OCC)
    return call(
        finish, shape((4, 4, 8, 128), F32), 1, 4, [pltpu.VMEM((8, 16, 128), F32)], (6 * 2 * 256 * 512 * 128, 2000000)
    )(occ, lab, r3, yr, chat)


def allowed(left, right, target):
    return (jnp.bitwise_xor(left, right) == target).astype(F32)


def dense(t, b, c, occ, vir, aux):
    o, v = occ_at(), vir_at()
    aux_mine = lax.dynamic_slice_in_dim(aux, o * 96, 96)
    vir_mine = lax.dynamic_slice_in_dim(vir, v * 8, 8)
    occ_mine = lax.dynamic_slice_in_dim(occ, o * 4, 4)
    own = b * allowed(vir_mine[None, :, None], vir[None, None, :], aux_mine[:, None, None])
    wide = lax.all_gather(b, VIR, axis=1, tiled=True)
    wide = wide * allowed(vir[None, :, None], vir[None, None, :], aux_mine[:, None, None])
    pairs = lax.all_gather(t, OCC, axis=1, tiled=True)
    inter = jnp.einsum("qac,qbd->acbd", own, wide, precision=HIGHEST)
    part = jnp.einsum("ijcd,acbd->ijab", lax.all_gather(pairs, VIR, axis=2, tiled=True), inter, precision=HIGHEST)
    total = lax.psum_scatter(part, OCC, scatter_dimension=1, tiled=True)
    swapped = lax.all_to_all(t, VIR, split_axis=3, concat_axis=2, tiled=True)
    u = 2.0 * t - jnp.transpose(swapped, (0, 1, 3, 2))
    cw = lax.all_gather(c, VIR, axis=2, tiled=True)
    cw = cw * allowed(occ_mine[None, :, None], vir[None, None, :], aux[:, None, None])
    y = lax.psum(jnp.einsum("ikac,qkc->iaq", u, cw, precision=HIGHEST), OCC)
    return total + jnp.einsum("iaq,qjb->ijab", y, cw, precision=HIGHEST)


def shards(t, b, c, occ, vir, aux):
    fast = folded(t, b, c, occ, vir, aux)
    member = aux.reshape(1, 8, 96) == jnp.arange(NG, dtype=jnp.int32).reshape(NG, 1, 1)
    count = jnp.sum(member.astype(jnp.int32), axis=2)
    fits = (jnp.max(count) <= SL) & (jnp.max(jnp.sum(count, axis=1)) <= SG)
    return lax.cond(fits, lambda *_: fast, dense, t, b, c, occ, vir, aux)


def solution(mesh):
    fine = Mesh(mesh.devices.reshape(2, 4, 4, 2, 2), ("yh", "x", "z", "yl", "core"))
    placed = (P(None, OCC, VIR, None), P(OCC, VIR, None), P(None, OCC, VIR), P(), P(), P())
    return jax.shard_map(shards, mesh=fine, in_specs=placed, out_specs=P(None, OCC, VIR, None), check_vma=False)
```

time: 343 us -> 125 us (0.36)
  matrix products: 163 us -> 0 us
  waiting for transfers between devices: 103 us -> 35 us
  Pallas kernels: 0 us -> 27.7 us
  blocking collectives: 30.4 us -> 21.9 us
  local copies, waits for them, and re-layouts: 12 us -> 5.13 us
  other arithmetic: 7.51 us -> 2.98 us
  starting transfers between devices: 12.8 us -> 16.6 us
    dot_general x4 -> x0, matrix products: 163 us -> none  [the longest x1 98.1 us: shards(): jnp.einsum('ijcd,acbd->ijab', lax.all_gather(pair_all, 'vir', axis=2, til...]
    reduce_scatter x1 -> x0, waiting for transfers between devices: 68.5 us -> none  [shards(): lax.psum_scatter(partial_sum, 'occ', scatter_dimension=1, tiled=True)]
    all_to_all x1 -> x3, waiting for transfers between devices: 0.54 us -> 35 us  [swap(): return lax.all_to_all(x, axes, 0, 0, tiled=True)]
    all_gather x3 -> x0, waiting for transfers between devices: 32.1 us -> none  [the longest x1 32.1 us: shards(): vv_wide = lax.all_gather(vv_factors, 'vir', axis=1, tiled=True)]
    all_gather x1 -> x0, blocking collectives: 30.4 us -> none  [shards(): pair_all = lax.all_gather(amplitudes, 'occ', axis=1, tiled=True)]
    pallas_call x0 -> x7, Pallas kernels: none -> 27.7 us  [the longest x1 9.66 us: folded(): call(ladder, shape((8, 8, 16, 128), F32), 1, 4, [pltpu.VMEM((16, 16, 8, 1...]
    all_to_all x0 -> x1, blocking collectives: none -> 21.9 us  [swap(): return lax.all_to_all(x, axes, 0, 0, tiled=True)]
    mul x2 -> x0, other arithmetic: 4.45 us -> none  [the longest x1 3.29 us: shards(): vv_wide * allowed(vir_irreps[None, :, None], vir_irreps[None, None, :], a...]
  transfers between devices with their start and end apart: 6 -> 4, of which waited for: 3 -> 3; matrix products, arithmetic and copies ran while one was open for 52% -> 2% of each run, Pallas kernels for 0% -> 8%
where the time goes in v1:
time: 125 us; the launch traced here: 124 us
  waiting for transfers between devices  35 us (28%)
  Pallas kernels  27.7 us (22%)
  blocking collectives  21.9 us (18%)
  starting transfers between devices  16.6 us (13%)
  between operations  14.7 us (12%)
  local copies, waits for them, and re-layouts  5.13 us (4%)
  other arithmetic  2.98 us (2%)
    all_to_all x3, waiting for transfers between devices, swap(): return lax.all_to_all(x, axes, 0, 0, tiled=True)  35 us
    all_to_all x1, blocking collectives, swap(): return lax.all_to_all(x, axes, 0, 0, tiled=True)  21.9 us
    all_to_all x3, starting transfers between devices, swap(): return lax.all_to_all(x, axes, 0, 0, tiled=True)  14.5 us
    pallas_call x1, Pallas kernels, folded(): call(ladder, shape((8, 8, 16, 128), F32), 1, 4, [pltpu.VMEM((16, 16, 8, 1...  9.66 us
    pallas_call x1, Pallas kernels, folded(): call(refold_rows, shape((384, 1024), BF16), 1, 2, [pltpu.VMEM((2048, 128)...  3.87 us
    pallas_call x1, Pallas kernels, folded(): call(cycle_first, (shape((8, 256, 128), F32), shape((512, 128), F32)), 1,...  3.64 us
    pallas_call x1, Pallas kernels, folded(): call(refold_own, shape((8, 304, 128), F32), 1, 4, [pltpu.VMEM((2048, 128)...  3.09 us
    unnamed x22, local copies, waits for them, and re-layouts  2.97 us
  transfers between devices with their start and end apart: 4, of which 3 were waited for; matrix products, arithmetic and copies ran while one was open for 2% of the time, Pallas kernels for 8%

profile of v1, /device:TPU:1, one launch (start us, length us, event | category | flops | bytes accessed | tf_op | source)
XLA Modules:
  0.0 124.0 jit_solution(8373628110216130027)
XLA Ops:
  6.5 0.8 eq.26
  7.4 0.7 pad_bitcast_fusion
  8.1 1.3 %fusion.40.lab_ref = s32[16,128]{1,0:T(8,128)} fusion(s32[8,96]{1,0:T(8,128)S(1)} %eq.26, s32[1,128]{1,0:T(1,128)S(1)} %pad_bitcast_fusion, s32[1,128]{1,0:T(1,128)} %bitcast.67, s32[16]{0:T(128)S(1)} %pad.13.clone), kind=kLoop, calls=%fused_computation.41 | loop fusion | flops 10240 | bytes 12352 | tf_op jit(solution)/shard_map/concatenate | solution.py:264
  9.4 2.8 %shard_map.66 = f32[8,208,128]{2,1,0:T(8,128)} custom-call(s32[128]{0:T(128)} %vir_s.9, s32[16,128]{1,0:T(8,128)} %fusion.40.lab_ref, f32[96,8,128]{2,1,0:T(8,128)} %b_ref.1, f32[4,4,8,128]{3,2,1,0:T(8,128)} %t_ref.5), custom_call_target="tpu_custom_call" | custom-call | flops 9437184 | bytes 1300000 | tf_op jit(solution)/shard_map/pallas_call | solution.py:266
  12.2 7.5 %all-to-all-start.1 = ((f32[8,208,128]{2,1,0:T(8,128)}), f32[8,208,128]{2,1,0:T(8,128)S(1)}, u32[]{:S(2)}, u32[]{:S(2)}) async-start(f32[8,208,128]{2,1,0:T(8,128)} %shard_map.66), calls=%async_computation.2 | async-start | bytes 1703936 | tf_op jit(solution)/shard_map/all_to_all | solution.py:258
  19.7 0.6 reshape.103.aux_ref
  20.3 2.0 %shard_map.68 = (f32[32,128]{1,0:T(8,128)}, f32[128,128]{1,0:T(8,128)}) custom-call(s32[128]{0:T(128)S(1)} %copy-done.13, s32[32]{0:T(128)S(1)} %copy-done.14, s32[1,768]{1,0:T(1,128)} %reshape.103.aux_ref, f32[4,8,768]{2,1,0:T(8,128)S(1)} %bitcast.66, f32[4,4,8,128]{3,2,1,0:T(8,128)S(1)} %copy-done.5), custom_call_target="tpu_custom_call" | custom-call | flops 22020096 | bytes 300000 | tf_op jit(solution)/shard_map/pallas_call | solution.py:271
  22.3 12.6 %all-to-all-done.1.r1_ref = f32[8,208,128]{2,1,0:T(8,128)S(1)} async-done(((f32[8,208,128]{2,1,0:T(8,128)}), f32[8,208,128]{2,1,0:T(8,128)S(1)}, u32[]{:S(2)}, u32[]{:S(2)}) %all-to-all-start.1) | async-done | bytes 852000 | tf_op jit(solution)/shard_map/all_to_all | solution.py:258
  34.9 0.9 copy-done.4
  35.8 3.1 %shard_map.69 = f32[8,304,128]{2,1,0:T(8,128)} custom-call(s32[128]{0:T(128)S(1)} %copy-done.13, s32[16,128]{1,0:T(8,128)} %fusion.40.lab_ref, f32[8,208,128]{2,1,0:T(8,128)} %copy-done.4, f32[32,128]{1,0:T(8,128)} %get-tuple-element.31.ch_ref, f32[128,128]{1,0:T(8,128)} %get-tuple-element.32.sw_ref), custom_call_target="tpu_custom_call" | custom-call | flops 134217728 | bytes 2300000 | tf_op jit(solution)/shard_map/pallas_call | solution.py:274
  38.9 21.9 %all_to_all.34.r2_ref = f32[8,304,128]{2,1,0:T(8,128)S(1)} all-to-all(f32[8,304,128]{2,1,0:T(8,128)} %shard_map.69), channel_id=1, replica_groups=mesh['yh'=2,'x'=4,'z'=4,'yl'=2,'core'=2] {'z','yl'}, dimensions={0} | all-to-all | bytes 2490368 | tf_op jit(solution)/shard_map/all_to_all | solution.py:258
  60.7 2.1 %collective-permute-start = (f32[8,304,128]{2,1,0:T(8,128)S(1)}, f32[8,304,128]{2,1,0:T(8,128)S(1)}, u32[]{:S(2)}, u32[]{:S(2)}) collective-permute-start(f32[8,304,128]{2,1,0:T(8,128)S(1)} %all_to_all.34.r2_ref), channel_id=1, source_target_pairs={{0,1},{1,0},{2,3},{3,2},{4,5},{5,4},{6,7},{7,6},{8,9},{9,8},{10,11... | collective-permute-start | bytes 3735560 | tf_op jit(solution)/shard_map/ppermute | solution.py:282
  62.8 3.9 %shard_map.67.b1_ref = bf16[384,1024]{1,0:T(8,128)(2,1)} custom-call(s32[128]{0:T(128)S(1)} %copy-done.13, s32[16,128]{1,0:T(8,128)} %fusion.40.lab_ref, f32[8,208,128]{2,1,0:T(8,128)} %copy-done.4), custom_call_target="tpu_custom_call" | custom-call | flops 1073741824 | bytes 1700000 | tf_op jit(solution)/shard_map/pallas_call | solution.py:279
  66.7 1.0 copy-done.8
  67.7 9.7 %shard_map.70 = f32[8,8,16,128]{3,2,1,0:T(8,128)} custom-call(s32[128]{0:T(128)S(1)} %copy-done.13, s32[16,128]{1,0:T(8,128)} %fusion.40.lab_ref, bf16[384,1024]{1,0:T(8,128)(2,1)} %shard_map.67.b1_ref, f32[8,304,128]{2,1,0:T(8,128)} %copy-done.1, f32[8,304,128]{2,1,0:T(8,128)} %copy-done.8), custom_call_target="tpu_custom_call" | custom-call | flops 3221225472 | bytes 4000000 | tf_op jit(solution)/shard_map/pallas_call | solution.py:288
  77.4 3.5 %all-to-all-start.3 = ((f32[8,8,16,128]{3,2,1,0:T(8,128)}), f32[8,8,16,128]{3,2,1,0:T(8,128)S(1)}, u32[]{:S(2)}, u32[]{:S(2)}) async-start(f32[8,8,16,128]{3,2,1,0:T(8,128)} %shard_map.70), calls=%async_computation.4 | async-start | bytes 1048576 | tf_op jit(solution)/shard_map/all_to_all | solution.py:258
  80.9 3.6 %shard_map.71 = (f32[8,256,128]{2,1,0:T(8,128)}, f32[512,128]{1,0:T(8,128)}) custom-call(s32[32]{0:T(128)S(1)} %copy-done.14, s32[16,128]{1,0:T(8,128)} %fusion.40.lab_ref, f32[8,304,128]{2,1,0:T(8,128)} %copy-done.1, f32[8,304,128]{2,1,0:T(8,128)} %copy-done.8, f32[4,4,8,128]{3,2,1,0:T(8,128)S(1)} %copy-done.5), custom_call_target="tpu_custom_call" | custom-call | flops 201326592 | bytes 4000000 | tf_op jit(solution)/shard_map/pallas_call | solution.py:283
  84.5 8.1 %all-to-all-done.3.r3_ref = f32[8,8,16,128]{3,2,1,0:T(8,128)S(1)} async-done(((f32[8,8,16,128]{3,2,1,0:T(8,128)}), f32[8,8,16,128]{3,2,1,0:T(8,128)S(1)}, u32[]{:S(2)}, u32[]{:S(2)}) %all-to-all-start.3) | async-done | bytes 524320 | tf_op jit(solution)/shard_map/all_to_all | solution.py:258
  92.6 3.6 %all-to-all-start.4 = ((f32[8,256,128]{2,1,0:T(8,128)}), f32[8,256,128]{2,1,0:T(8,128)S(1)}, u32[]{:S(2)}, u32[]{:S(2)}) async-start(f32[8,256,128]{2,1,0:T(8,128)} %get-tuple-element.33), calls=%async_computation.5 | async-start | bytes 2097152 | tf_op jit(solution)/shard_map/all_to_all | solution.py:258
  96.5 0.6 reduce_max.18
  97.2 0.7 reduce_max.19
  99.1 14.3 %all-to-all-done.4.y_ref = f32[8,256,128]{2,1,0:T(8,128)S(1)} async-done(((f32[8,256,128]{2,1,0:T(8,128)}), f32[8,256,128]{2,1,0:T(8,128)S(1)}, u32[]{:S(2)}, u32[]{:S(2)}) %all-to-all-start.4) | async-done | bytes 1048608 | tf_op jit(solution)/shard_map/all_to_all | solution.py:258
  113.5 1.0 copy-done.2
  114.5 2.7 %shard_map.72 = f32[4,4,8,128]{3,2,1,0:T(8,128)} custom-call(s32[32]{0:T(128)S(1)} %copy-done.14, s32[16,128]{1,0:T(8,128)} %fusion.40.lab_ref, f32[8,8,16,128]{3,2,1,0:T(8,128)} %copy-done.7, f32[8,256,128]{2,1,0:T(8,128)} %copy-done.2, f32[512,128]{1,0:T(8,128)} %get-tuple-element.34.chat_ref), custom_call_target="tpu_custom_call" | custom-call | flops 201326592 | bytes 2000000 | tf_op jit(solution)/shard_map/pallas_call | solution.py:300
  (24 shorter events, 0.5 us)
Async XLA Ops:
  6.5 13.1 %copy-start.12 = (s32[768]{0:T(1024)S(1)}, s32[768]{0:T(1024)}, u32[]{:S(2)}) copy-start(s32[768]{0:T(1024)} %param.13) | copy-start | bytes 9220
  6.5 13.7 %copy-start.14 = (s32[32]{0:T(128)S(1)}, s32[32]{0:T(128)}, u32[]{:S(2)}) copy-start(s32[32]{0:T(128)} %occ_s.5) | copy-start | bytes 388
  6.5 13.7 %copy-start.13 = (s32[128]{0:T(128)S(1)}, s32[128]{0:T(128)}, u32[]{:S(2)}) copy-start(s32[128]{0:T(128)} %vir_s.9) | copy-start | bytes 1540
  6.5 13.7 %copy-start.5 = (f32[4,4,8,128]{3,2,1,0:T(8,128)S(1)}, f32[4,4,8,128]{3,2,1,0:T(8,128)}, u32[]{:S(2)}) copy-start(f32[4,4,8,128]{3,2,1,0:T(8,128)} %t_ref.5) | copy-start | bytes 196612
  6.5 13.7 %copy-start.11 = (f32[768,4,8]{0,2,1:T(8,128)S(1)}, f32[768,4,8]{0,2,1:T(8,128)}, u32[]{:S(2)}) copy-start(f32[768,4,8]{0,2,1:T(8,128)} %param.10) | copy-start | bytes 294916
  12.2 22.7 %all-to-all-start.1 = ((f32[8,208,128]{2,1,0:T(8,128)}), f32[8,208,128]{2,1,0:T(8,128)S(1)}, u32[]{:S(2)}, u32[]{:S(2)}) async-start(f32[8,208,128]{2,1,0:T(8,128)} %shard_map.66), calls=%async_computation.2 | async-start | bytes 1703936 | tf_op jit(solution)/shard_map/all_to_all | solution.py:258
  34.9 0.9 copy-start.4
  60.7 6.0 %copy-start.1 = (f32[8,304,128]{2,1,0:T(8,128)}, f32[8,304,128]{2,1,0:T(8,128)S(1)}, u32[]{:S(2)}) copy-start(f32[8,304,128]{2,1,0:T(8,128)S(1)} %all_to_all.34.r2_ref) | copy-start | bytes 3735556
  60.7 6.0 %collective-permute-start = (f32[8,304,128]{2,1,0:T(8,128)S(1)}, f32[8,304,128]{2,1,0:T(8,128)S(1)}, u32[]{:S(2)}, u32[]{:S(2)}) collective-permute-start(f32[8,304,128]{2,1,0:T(8,128)S(1)} %all_to_all.34.r2_ref), channel_id=1, source_target_pairs={{0,1},{1,0},{2,3},{3,2},{4,5},{5,4},{6,7},{7,6},{8,9},{9,8},{10,11... | collective-permute-start | bytes 3735560 | tf_op jit(solution)/shard_map/ppermute | solution.py:282
  66.7 1.0 copy-start.8
  77.4 15.2 %all-to-all-start.3 = ((f32[8,8,16,128]{3,2,1,0:T(8,128)}), f32[8,8,16,128]{3,2,1,0:T(8,128)S(1)}, u32[]{:S(2)}, u32[]{:S(2)}) async-start(f32[8,8,16,128]{3,2,1,0:T(8,128)} %shard_map.70), calls=%async_computation.4 | async-start | bytes 1048576 | tf_op jit(solution)/shard_map/all_to_all | solution.py:258
  84.5 29.9 %copy-start.3 = (f32[96,8,128]{2,1,0:T(8,128)S(1)}, f32[96,8,128]{2,1,0:T(8,128)}, u32[]{:S(2)}) copy-start(f32[96,8,128]{2,1,0:T(8,128)} %b_ref.1) | copy-start | bytes 1179652
  92.6 20.9 %copy-start.7 = (f32[8,8,16,128]{3,2,1,0:T(8,128)}, f32[8,8,16,128]{3,2,1,0:T(8,128)S(1)}, u32[]{:S(2)}) copy-start(f32[8,8,16,128]{3,2,1,0:T(8,128)S(1)} %all-to-all-done.3.r3_ref) | copy-start | bytes 1572868
  92.6 20.9 %all-to-all-start.4 = ((f32[8,256,128]{2,1,0:T(8,128)}), f32[8,256,128]{2,1,0:T(8,128)S(1)}, u32[]{:S(2)}, u32[]{:S(2)}) async-start(f32[8,256,128]{2,1,0:T(8,128)} %get-tuple-element.33), calls=%async_computation.5 | async-start | bytes 2097152 | tf_op jit(solution)/shard_map/all_to_all | solution.py:258
  113.5 1.0 copy-start.2

commit v2 on v1

--- a/solution.py
+++ b/solution.py
@@ -18,7 +18,7 @@
 NG = 8
 VMEM = pl.BlockSpec(memory_space=pltpu.VMEM)
 SMEM = pl.BlockSpec(memory_space=pltpu.SMEM)
-LIMIT = 56 * 2**20
+LIMIT = 14 * 2**20
 
 
 def occ_at():
@@ -58,14 +58,31 @@
     )
 
 
-def fold_local(vir_s, lab_ref, b_ref, t_ref, out_ref, roll_ref):
+def aux_block(aux_ref, block):
+    row, skip = lax.div(3 * block, 4), 32 * lax.rem(3 * block, 4)
+    first = jnp.broadcast_to(aux_ref[pl.ds(row, 1), :], (8, 128))
+    second = jnp.broadcast_to(aux_ref[pl.ds(jnp.minimum(row + 1, 5), 1), :], (8, 128))
+    lane = iota((8, 128), 1)
+    shift = lax.rem(128 - skip, 128)
+    joined = jnp.where(lane < 128 - skip, pltpu.roll(first, shift, 1), pltpu.roll(second, shift, 1))
+    return jnp.where(lane < 96, joined, NG)
+
+
+def aux_blocks(aux_ref):
+    rows = jnp.zeros((8, 128), jnp.int32)
+    for block in range(8):
+        rows = jnp.where(iota((8, 128), 0) == block, aux_block(aux_ref, jnp.int32(block)), rows)
+    return rows
+
+
+def fold_local(vir_s, aux_ref, vir_ref, b_ref, t_ref, out_ref, roll_ref):
     o, v = occ_at(), vir_at()
-    q_lane = jnp.broadcast_to(lab_ref[pl.ds(o, 1), :], (128, 128))
+    q_lane = jnp.broadcast_to(aux_block(aux_ref, o)[0:1], (128, 128))
     q_sub = jnp.transpose(q_lane)
     same = (q_sub == q_lane) & (iota((128, 128), 0) < iota((128, 128), 1))
     rank = jnp.sum(same.astype(F32), axis=0, keepdims=True)
     pick = (rank == iota((SL, 128), 0).astype(F32)).astype(F32)[:, :96].astype(BF16)
-    y_row = lab_ref[8:9, :]
+    y_row = vir_ref[...]
     for x in range(8):
         keep = (y_row ^ vir_s[v * 8 + x]) == q_sub[:96]
         hi, lo = split(jnp.where(keep, b_ref[:, x, :], 0.0))
@@ -83,9 +100,15 @@
         out_ref[peer, 8 * SL : 8 * SL + 16, :] = block
 
 
-def fold_ov(vir_s, occ_s, aux_ref, c_ref, t_ref, ch_ref, sw_ref):
+def fold_ov(vir_s, occ_s, aux_ref, c_ref, t_ref, ch_ref, sw_ref, fits_ref):
     o, v = occ_at(), vir_at()
-    aux = aux_ref[...]
+    rows = aux_blocks(aux_ref)
+    over = jnp.zeros((8, 1), F32)
+    for g in range(NG):
+        count = jnp.sum((rows == g).astype(F32), axis=1, keepdims=True)
+        over = jnp.maximum(over, jnp.maximum(count - SL, jnp.sum(count, axis=0, keepdims=True) - SG))
+    fits_ref[0] = (jnp.max(over) < 0.5).astype(jnp.int32)
+    aux = jnp.concatenate([aux_ref[n : n + 1, :] for n in range(6)], axis=1)
     member = (aux == iota((NG, 768), 0)).astype(F32)
     before = (iota((768, 768), 0) < iota((768, 768), 1)).astype(F32).astype(BF16)
     rank = jnp.sum(member * dot(member.astype(BF16), before), axis=0, keepdims=True)
@@ -100,9 +123,9 @@
     sw_ref[...] = jnp.transpose(t_ref[...].reshape(128, 128))
 
 
-def place(lab_ref, place_ref):
+def place(aux_ref, place_ref):
     lane = iota((SL, 128), 1).astype(F32) - iota((SL, 128), 0).astype(F32)
-    aux = lab_ref[0:8, :]
+    aux = aux_blocks(aux_ref)
     for g in range(NG):
         count = jnp.sum((aux == g).astype(F32), axis=1, keepdims=True)
         start = jnp.zeros((1, 1), F32)
@@ -113,11 +136,11 @@
         place_ref[g * 256 + 8 * SL : (g + 1) * 256, :] = jnp.zeros((256 - 8 * SL, 128), F32)
 
 
-def refold_own(vir_s, lab_ref, r1_ref, ch_ref, sw_ref, out_ref, place_ref, row_ref):
+def refold_own(vir_s, aux_ref, vir_ref, r1_ref, ch_ref, sw_ref, out_ref, place_ref, row_ref):
     o, v = occ_at(), vir_at()
-    place(lab_ref, place_ref)
+    place(aux_ref, place_ref)
     group = iota((1, 128), 1) // 16
-    y_row = jnp.broadcast_to(lab_ref[8:9, :], (8, 128))
+    y_row = jnp.broadcast_to(vir_ref[...], (8, 128))
     mine = jnp.zeros((8 * SL, 128), F32)
     label = jnp.zeros((8, 128), jnp.int32)
     for x in range(8):
@@ -149,13 +172,13 @@
         out_ref[peer, 288:304, :] = sw_ref[16 * peer : 16 * peer + 16, :]
 
 
-def refold_rows(vir_s, lab_ref, r1_ref, out_ref, place_ref):
+def refold_rows(vir_s, aux_ref, vir_ref, r1_ref, out_ref, place_ref):
     v = vir_at()
-    place(lab_ref, place_ref)
+    place(aux_ref, place_ref)
     spread = jnp.concatenate(
         [jnp.transpose(place_ref[128 * n : 128 * n + 128, :]).astype(BF16) for n in range(2 * NG)], axis=1
     )
-    y_row = lab_ref[8:9, :]
+    y_row = vir_ref[...]
     pad = jnp.zeros((256 - 8 * SL, 128), F32)
     for x in range(8):
         label = y_row ^ vir_s[v * 8 + x]
@@ -173,7 +196,7 @@
         out_ref[256:384, x * 128 : x * 128 + 128] = hi
 
 
-def cycle_first(occ_s, lab_ref, r2_ref, o2_ref, t_ref, y_ref, chat_ref, got_ref):
+def cycle_first(occ_s, vir_ref, r2_ref, o2_ref, t_ref, y_ref, chat_ref, got_ref):
     o, core = occ_at(), lax.axis_index("core")
     for p in range(8):
         got_ref[2 * p + core] = r2_ref[p, 256:304, :]
@@ -194,21 +217,20 @@
             row.append(2.0 * t_ref[i, k] - swapped)
         u.append(jnp.concatenate(row, axis=1))
     u = jnp.concatenate(u, axis=0)
-    label = jnp.concatenate([lab_ref[8:9, :] ^ occ_s[o * 4 + k] for k in range(4)], axis=1)
+    label = jnp.concatenate([vir_ref[...] ^ occ_s[o * 4 + k] for k in range(4)], axis=1)
     rows = jnp.concatenate([jnp.where(label == g, u, 0.0) for g in range(NG)], axis=0)
     y = jnp.dot(rows, chat_ref[...], precision=HIGHEST, preferred_element_type=F32)
-    for peer in range(8):
-        y_ref[peer] = y
-
-
-def ladder(vir_s, lab_ref, b1_ref, r2_ref, o2_ref, out_ref, f_ref, t_ref, hi_ref, lo_ref, acc_ref):
+    y_ref[...] = y.reshape(8, 32, 128)
+
+
+def ladder(vir_s, vir_ref, b1_ref, r2_ref, o2_ref, out_ref, f_ref, t_ref, hi_ref, lo_ref, acc_ref):
     o, v, core = occ_at(), vir_at(), lax.axis_index("core")
     for ref, part in ((r2_ref, core), (o2_ref, 1 - core)):
         for p in range(8):
             f_ref[:, 2 * p + part] = ref[p, 0:128, :].reshape(16, 8, 128)
             t_ref[:, 2 * p + part] = ref[p, 128:256, :].reshape(16, 8, 128)
     acc_ref[...] = jnp.zeros_like(acc_ref)
-    c_lane = jnp.broadcast_to(lab_ref[8:9, :], (128, 128))
+    c_lane = jnp.broadcast_to(vir_ref[...], (128, 128))
     bc = jnp.transpose(c_lane) ^ c_lane
 
     def step(n, carry):
@@ -236,22 +258,29 @@
             out_ref[p, a] = rows[16 * p : 16 * p + 16, :]
 
 
-def finish(occ_s, lab_ref, r3_ref, y_ref, chat_ref, out_ref, sum_ref):
-    o = occ_at()
-    total = r3_ref[0]
+def join(p3_ref, y_ref, out_ref):
     y = y_ref[0]
     for p in range(1, 8):
-        total = total + r3_ref[p]
         y = y + y_ref[p]
+    for p in range(8):
+        out_ref[p, 0:128, :] = p3_ref[p].reshape(128, 128)
+        out_ref[p, 128:160, :] = y
+
+
+def finish(occ_s, vir_ref, r3_ref, chat_ref, out_ref, sum_ref):
+    o = occ_at()
+    total = r3_ref[0, 0:128, :]
+    for p in range(1, 8):
+        total = total + r3_ref[p, 0:128, :]
     sum_ref[...] = total
-    z = dot_t(y, chat_ref[...], HIGHEST)
+    z = dot_t(jnp.concatenate([r3_ref[p, 128:160, :] for p in range(8)], axis=0), chat_ref[...], HIGHEST)
     for j in range(4):
-        label = lab_ref[8:9, :] ^ occ_s[o * 4 + j]
+        label = vir_ref[...] ^ occ_s[o * 4 + j]
         part = jnp.zeros((32, 128), F32)
         for g in range(NG):
             part = jnp.where(label == g, z[g * 32 : g * 32 + 32, j * 128 : j * 128 + 128], part)
         for i in range(4):
-            out_ref[i, j] = sum_ref[:, i * 4 + j, :] + part[8 * i : 8 * i + 8, :]
+            out_ref[i, j] = sum_ref[pl.ds(i * 4 + j, 8, stride=16), :] + part[8 * i : 8 * i + 8, :]
 
 
 def swap(x, axes):
@@ -259,31 +288,34 @@
 
 
 def folded(t, b, c, occ, vir, aux):
-    aux8 = jnp.pad(aux.reshape(8, 96), ((0, 0), (0, 32)), constant_values=NG)
-    rest = jnp.stack([vir, jnp.pad(occ, (0, 96), constant_values=NG)])
-    lab = jnp.concatenate([aux8, rest, jnp.zeros((6, 128), jnp.int32)], axis=0)
+    aux, row = aux.reshape(6, 128), vir.reshape(1, 128)
     shape = jax.ShapeDtypeStruct
     p1 = call(
-        fold_local, shape((8, 8 * SL + 16, 128), F32), 1, 3, [pltpu.VMEM((8, 16, 8, 128), F32)],
+        fold_local, shape((8, 8 * SL + 16, 128), F32), 1, 4, [pltpu.VMEM((8, 16, 8, 128), F32)],
         (2 * 2 * 24 * 96 * 1024, 1300000),
-    )(vir, lab, b, t)
+    )(vir, aux, row, b, t)
     r1 = swap(p1, OCC)
-    ch, sw = call(
-        fold_ov, (shape((32, 128), F32), shape((128, 128), F32)), 2, 3, (), (2 * 8 * 768 * 768 + 4 * 32 * 768 * 128, 300000)
-    )(vir, occ, aux.reshape(1, 768), jnp.transpose(c, (1, 2, 0)), t)
+    ch, sw, fits = pl.pallas_call(
+        fold_ov,
+        out_shape=(shape((32, 128), F32), shape((128, 128), F32), shape((1,), jnp.int32)),
+        in_specs=[SMEM, SMEM, VMEM, VMEM, VMEM],
+        out_specs=(VMEM, VMEM, SMEM),
+        compiler_params=pltpu.CompilerParams(vmem_limit_bytes=LIMIT),
+        cost_estimate=pl.CostEstimate(flops=2 * 8 * 768 * 768, bytes_accessed=300000, transcendentals=0),
+    )(vir, occ, aux, jnp.transpose(c, (1, 2, 0)), t)
     p2 = call(
-        refold_own, shape((8, 304, 128), F32), 1, 4, [pltpu.VMEM((2048, 128), F32), pltpu.VMEM((2, 128, 128), F32)],
+        refold_own, shape((8, 304, 128), F32), 1, 5, [pltpu.VMEM((2048, 128), F32), pltpu.VMEM((2, 128, 128), F32)],
         (2 * 256 * 2048 * 128, 2300000),
-    )(vir, lab, r1, ch, sw)
+    )(vir, aux, row, r1, ch, sw)
     r2 = swap(p2, ZY)
     b1 = call(
-        refold_rows, shape((384, 1024), BF16), 1, 2, [pltpu.VMEM((2048, 128), F32)], (2 * 128 * 2048 * 2048, 1700000)
-    )(vir, lab, r1)
+        refold_rows, shape((384, 1024), BF16), 1, 3, [pltpu.VMEM((2048, 128), F32)], (2 * 128 * 2048 * 2048, 1700000)
+    )(vir, aux, row, r1)
     o2 = lax.ppermute(r2, "core", [(0, 1), (1, 0)])
     yp, chat = call(
-        cycle_first, (shape((8, 256, 128), F32), shape((512, 128), F32)), 1, 4, [pltpu.VMEM((16, 48, 128), F32)],
+        cycle_first, (shape((8, 32, 128), F32), shape((512, 128), F32)), 1, 4, [pltpu.VMEM((16, 48, 128), F32)],
         (6 * 2 * 256 * 512 * 128, 4000000),
-    )(occ, lab, r2, o2, t)
+    )(occ, row, r2, o2, t)
     yr = swap(yp, OCC)
     p3 = call(
         ladder, shape((8, 8, 16, 128), F32), 1, 4,
@@ -295,11 +327,12 @@
             pltpu.VMEM((1024, 128), F32),
         ],
         (6 * 2048 * 1024 * 256, 4000000),
-    )(vir, lab, b1, r2, o2)
-    r3 = swap(p3, OCC)
-    return call(
-        finish, shape((4, 4, 8, 128), F32), 1, 4, [pltpu.VMEM((8, 16, 128), F32)], (6 * 2 * 256 * 512 * 128, 2000000)
-    )(occ, lab, r3, yr, chat)
+    )(vir, row, b1, r2, o2)
+    r3 = swap(call(join, shape((8, 160, 128), F32), 0, 2, (), (0, 1300000))(p3, yr), OCC)
+    out = call(
+        finish, shape((4, 4, 8, 128), F32), 1, 3, [pltpu.VMEM((128, 128), F32)], (6 * 2 * 256 * 512 * 128, 2000000)
+    )(occ, row, r3, chat)
+    return out, fits
 
 
 def allowed(left, right, target):
@@ -327,11 +360,8 @@
 
 
 def shards(t, b, c, occ, vir, aux):
-    fast = folded(t, b, c, occ, vir, aux)
-    member = aux.reshape(1, 8, 96) == jnp.arange(NG, dtype=jnp.int32).reshape(NG, 1, 1)
-    count = jnp.sum(member.astype(jnp.int32), axis=2)
-    fits = (jnp.max(count) <= SL) & (jnp.max(jnp.sum(count, axis=1)) <= SG)
-    return lax.cond(fits, lambda *_: fast, dense, t, b, c, occ, vir, aux)
+    fast, fits = folded(t, b, c, occ, vir, aux)
+    return lax.cond(fits[0] > 0, lambda *_: fast, dense, t, b, c, occ, vir, aux)
 
 
 def solution(mesh):

time: 125 us -> 105 us (0.84)
  waiting for transfers between devices: 35 us -> 26.1 us
  Pallas kernels: 27.7 us -> 20.7 us
  local copies, waits for them, and re-layouts: 5.13 us -> 1.89 us
  other arithmetic: 2.98 us -> 0 us
  starting transfers between devices: 16.6 us -> 19.5 us
    all_to_all x3, waiting for transfers between devices: 35 us -> 25.9 us  [swap(): return lax.all_to_all(x, axes, 0, 0, tiled=True)]
    pallas_call x6 -> x7, Pallas kernels: 18 us -> 13.2 us  [the longest x1 2.92 us: folded(): call(fold_local, shape((8, 8 * SL + 16, 128), F32), 1, 4, [pltpu.VMEM((8,...]
    all_to_all x3, starting transfers between devices: 14.5 us -> 17.4 us  [swap(): return lax.all_to_all(x, axes, 0, 0, tiled=True)]
    pallas_call x1, Pallas kernels: 9.66 us -> 7.49 us  [folded(): call(ladder, shape((8, 8, 16, 128), F32), 1, 4, [pltpu.VMEM((16, 16, 8, 1...]
    concatenate x1 -> x0, other arithmetic: 1.32 us -> none  [folded(): lab = jnp.concatenate([aux8, rest, jnp.zeros((6, 128), jnp.int32)], axis=0)]
    reduce_max x2 -> x0, other arithmetic: 1.3 us -> none  [shards(): fits = (jnp.max(count) <= SL) & (jnp.max(jnp.sum(count, axis=1)) <= SG)]
    unnamed x22 -> x24, local copies, waits for them, and re-layouts: 2.97 us -> 1.89 us
  transfers between devices with their start and end apart: 4 -> 4, of which waited for: 3 -> 3; matrix products, arithmetic and copies ran while one was open for 2% -> 0% of each run, Pallas kernels for 8% -> 11%
where the time goes in v2:
time: 105 us; the launch traced here: 104 us
  waiting for transfers between devices  26.1 us (25%)
  blocking collectives  21.7 us (21%)
  Pallas kernels  20.7 us (20%)
  starting transfers between devices  19.5 us (19%)
  between operations  14.2 us (14%)
  local copies, waits for them, and re-layouts  1.89 us (2%)
    all_to_all x3, waiting for transfers between devices, swap(): return lax.all_to_all(x, axes, 0, 0, tiled=True)  25.9 us
    all_to_all x1, blocking collectives, swap(): return lax.all_to_all(x, axes, 0, 0, tiled=True)  21.7 us
    all_to_all x3, starting transfers between devices, swap(): return lax.all_to_all(x, axes, 0, 0, tiled=True)  17.4 us
    pallas_call x1, Pallas kernels, folded(): call(ladder, shape((8, 8, 16, 128), F32), 1, 4, [pltpu.VMEM((16, 16, 8, 1...  7.49 us
    pallas_call x1, Pallas kernels, folded(): call(fold_local, shape((8, 8 * SL + 16, 128), F32), 1, 4, [pltpu.VMEM((8,...  2.92 us
    pallas_call x1, Pallas kernels, folded(): call(refold_rows, shape((384, 1024), BF16), 1, 3, [pltpu.VMEM((2048, 128)...  2.4 us
    pallas_call x1, Pallas kernels, folded(): call(cycle_first, (shape((8, 32, 128), F32), shape((512, 128), F32)), 1,...  2.16 us
  transfers between devices with their start and end apart: 4, of which 3 were waited for; matrix products, arithmetic and copies ran while one was open for 0% of the time, Pallas kernels for 11%

profile of v2, /device:TPU:1, one launch (start us, length us, event | category | flops | bytes accessed | tf_op | source)
XLA Modules:
  0.0 104.3 jit_solution(14916066308247378858)
XLA Ops:
  6.5 2.9 %shard_map.67 = f32[8,208,128]{2,1,0:T(8,128)} custom-call(s32[128]{0:T(128)} %vir_s.9, s32[6,128]{1,0:T(8,128)} %bitcast.67, s32[1,128]{1,0:T(1,128)} %bitcast.71, f32[96,8,128]{2,1,0:T(8,128)} %b_ref.1, f32[4,4,8,128]{3,2,1,0:T(8,128)} %t_ref.5), custom_call_target="tpu_custom_call" | custom-call | flops 9437184 | bytes 1300000 | tf_op jit(solution)/shard_map/pallas_call | solution.py:293
  9.5 7.5 %all-to-all-start.1 = ((f32[8,208,128]{2,1,0:T(8,128)}), f32[8,208,128]{2,1,0:T(8,128)S(1)}, u32[]{:S(2)}, u32[]{:S(2)}) async-start(f32[8,208,128]{2,1,0:T(8,128)} %shard_map.67), calls=%async_computation.2 | async-start | bytes 1703936 | tf_op jit(solution)/shard_map/all_to_all | solution.py:287
  17.0 0.0 copy-done.13
  17.0 1.7 %shard_map.66 = (f32[32,128]{1,0:T(8,128)S(1)}, f32[128,128]{1,0:T(8,128)S(1)}, s32[1]{0:T(128)}) custom-call(s32[128]{0:T(128)S(1)} %copy-done.14, s32[32]{0:T(128)S(1)} %copy-done.15, s32[6,128]{1,0:T(8,128)S(1)} %bitcast.68, f32[4,8,768]{2,1,0:T(8,128)S(1)} %bitcast.66, f32[4,4,8,128]{3,2,1,0:T(8,128)S(1)} %copy-done.6), custom_call_target="tpu_custom_call" | custom-call | flops 9437184 | bytes 300000 | tf_op jit(solution)/shard_map/pallas_call | solution.py:298
  18.7 13.5 %all-to-all-done.1.r1_ref = f32[8,208,128]{2,1,0:T(8,128)S(1)} async-done(((f32[8,208,128]{2,1,0:T(8,128)}), f32[8,208,128]{2,1,0:T(8,128)S(1)}, u32[]{:S(2)}, u32[]{:S(2)}) %all-to-all-start.1) | async-done | bytes 852000 | tf_op jit(solution)/shard_map/all_to_all | solution.py:287
  32.2 1.4 %shard_map.69 = f32[8,304,128]{2,1,0:T(8,128)S(1)} custom-call(s32[128]{0:T(128)S(1)} %copy-done.14, s32[6,128]{1,0:T(8,128)S(1)} %bitcast.69, s32[1,128]{1,0:T(1,128)S(1)} %bitcast.72, f32[8,208,128]{2,1,0:T(8,128)S(1)} %all-to-all-done.1.r1_ref, f32[32,128]{1,0:T(8,128)S(1)} %get-tuple-element.33.ch_ref, f32[128,128]{1,0:T(8,128)S(1)} %get-tuple-element.34.sw_ref), custom_call_target="tpu_custom_call" | custom-call | flops 134217728 | bytes 2300000 | tf_op jit(solution)/shard_map/pallas_call | solution.py:306
  33.6 21.7 %all_to_all.34.r2_ref = f32[8,304,128]{2,1,0:T(8,128)S(1)} all-to-all(f32[8,304,128]{2,1,0:T(8,128)S(1)} %shard_map.69), channel_id=1, replica_groups=mesh['yh'=2,'x'=4,'z'=4,'yl'=2,'core'=2] {'z','yl'}, dimensions={0} | all-to-all | bytes 2490368 | tf_op jit(solution)/shard_map/all_to_all | solution.py:287
  55.2 2.1 %collective-permute-start = (f32[8,304,128]{2,1,0:T(8,128)S(1)}, f32[8,304,128]{2,1,0:T(8,128)S(1)}, u32[]{:S(2)}, u32[]{:S(2)}) collective-permute-start(f32[8,304,128]{2,1,0:T(8,128)S(1)} %all_to_all.34.r2_ref), channel_id=1, source_target_pairs={{0,1},{1,0},{2,3},{3,2},{4,5},{5,4},{6,7},{7,6},{8,9},{9,8},{10,11... | collective-permute-start | bytes 3735560 | tf_op jit(solution)/shard_map/ppermute | solution.py:314
  57.3 2.4 %shard_map.68.b1_ref = bf16[384,1024]{1,0:T(8,128)(2,1)S(1)} custom-call(s32[128]{0:T(128)S(1)} %copy-done.14, s32[6,128]{1,0:T(8,128)S(1)} %bitcast.70, s32[1,128]{1,0:T(1,128)S(1)} %bitcast.73, f32[8,208,128]{2,1,0:T(8,128)S(1)} %all-to-all-done.1.r1_ref), custom_call_target="tpu_custom_call" | custom-call | flops 1073741824 | bytes 1700000 | tf_op jit(solution)/shard_map/pallas_call | solution.py:311
  59.7 0.1 collective-permute-done.o2_ref
  59.9 2.2 %shard_map.71 = (f32[8,32,128]{2,1,0:T(8,128)}, f32[512,128]{1,0:T(8,128)S(1)}) custom-call(s32[32]{0:T(128)S(1)} %copy-done.15, s32[1,128]{1,0:T(1,128)S(1)} %bitcast.74, f32[8,304,128]{2,1,0:T(8,128)S(1)} %all_to_all.34.r2_ref, f32[8,304,128]{2,1,0:T(8,128)S(1)} %collective-permute-done.o2_ref, f32[4,4,8,128]{3,2,1,0:T(8,128)S(1)} %copy-done.6), custom_call_target="tpu_custom_call" | custom-call | flops 201326592 | bytes 4000000 | tf_op jit(solution)/shard_map/pallas_call | solution.py:315
  62.1 0.7 copy-done
  62.8 3.4 %all-to-all-start.3 = ((f32[8,32,128]{2,1,0:T(8,128)}), f32[8,32,128]{2,1,0:T(8,128)S(1)}, u32[]{:S(2)}, u32[]{:S(2)}) async-start(f32[8,32,128]{2,1,0:T(8,128)} %get-tuple-element.35), calls=%async_computation.4 | async-start | bytes 262144 | tf_op jit(solution)/shard_map/all_to_all | solution.py:287
  66.2 1.1 %copy-done.3 = bf16[384,1024]{1,0:T(8,128)(2,1)S(1)} copy-done((bf16[384,1024]{1,0:T(8,128)(2,1)S(1)}, bf16[384,1024]{1,0:T(8,128)(2,1)}, u32[]{:S(2)}) %copy-start.3) | copy-done | bytes 786456
  67.3 7.5 %shard_map.70.p3_ref = f32[8,8,16,128]{3,2,1,0:T(8,128)S(1)} custom-call(s32[128]{0:T(128)S(1)} %copy-done.14, s32[1,128]{1,0:T(1,128)S(1)} %bitcast.75, bf16[384,1024]{1,0:T(8,128)(2,1)S(1)} %copy-done.3, f32[8,304,128]{2,1,0:T(8,128)S(1)} %all_to_all.34.r2_ref, f32[8,304,128]{2,1,0:T(8,128)S(1)} %collective-permute-done.o2_ref), custom_call_target="tpu_custom_call" | custom-call | flops 3221225472 | bytes 4000000 | tf_op jit(solution)/shard_map/pallas_call | solution.py:320
  74.8 0.0 copy-start.5
  74.8 0.0 copy-start.7
  74.8 0.0 copy-start.12
  74.8 0.0 all-to-all-done.3.y_ref
  74.8 0.9 shard_map.72
  75.7 6.6 %all-to-all-start.4 = ((f32[8,160,128]{2,1,0:T(8,128)}), f32[8,160,128]{2,1,0:T(8,128)S(1)}, u32[]{:S(2)}, u32[]{:S(2)}) async-start(f32[8,160,128]{2,1,0:T(8,128)} %shard_map.72), calls=%async_computation.5 | async-start | bytes 1310720 | tf_op jit(solution)/shard_map/all_to_all | solution.py:287
  83.0 12.4 %all-to-all-done.4.r3_ref = f32[8,160,128]{2,1,0:T(8,128)S(1)} async-done(((f32[8,160,128]{2,1,0:T(8,128)}), f32[8,160,128]{2,1,0:T(8,128)S(1)}, u32[]{:S(2)}, u32[]{:S(2)}) %all-to-all-start.4) | async-done | bytes 655392 | tf_op jit(solution)/shard_map/all_to_all | solution.py:287
  95.4 1.8 %shard_map.73 = f32[4,4,8,128]{3,2,1,0:T(8,128)} custom-call(s32[32]{0:T(128)S(1)} %copy-done.15, s32[1,128]{1,0:T(1,128)S(1)} %bitcast.76, f32[8,160,128]{2,1,0:T(8,128)S(1)} %all-to-all-done.4.r3_ref, f32[512,128]{1,0:T(8,128)S(1)} %copy-done.1), custom_call_target="tpu_custom_call" | custom-call | flops 201326592 | bytes 2000000 | tf_op jit(solution)/shard_map/pallas_call | solution.py:332
  97.2 0.2 conditional.1
  (18 shorter events, 0.0 us)
Async XLA Ops:
  6.5 10.4 %copy-start.14 = (s32[128]{0:T(128)S(1)}, s32[128]{0:T(128)}, u32[]{:S(2)}) copy-start(s32[128]{0:T(128)} %vir_s.9) | copy-start | bytes 1540
  6.5 10.4 %copy-start.13 = (s32[768]{0:T(1024)S(1)}, s32[768]{0:T(1024)}, u32[]{:S(2)}) copy-start(s32[768]{0:T(1024)} %param.13) | copy-start | bytes 9220
  6.5 10.4 %copy-start.6 = (f32[4,4,8,128]{3,2,1,0:T(8,128)S(1)}, f32[4,4,8,128]{3,2,1,0:T(8,128)}, u32[]{:S(2)}) copy-start(f32[4,4,8,128]{3,2,1,0:T(8,128)} %t_ref.5) | copy-start | bytes 196612
  6.5 10.4 %copy-start.11 = (f32[768,4,8]{0,2,1:T(8,128)S(1)}, f32[768,4,8]{0,2,1:T(8,128)}, u32[]{:S(2)}) copy-start(f32[768,4,8]{0,2,1:T(8,128)} %param.10) | copy-start | bytes 294916
  6.5 10.4 %copy-start.15 = (s32[32]{0:T(128)S(1)}, s32[32]{0:T(128)}, u32[]{:S(2)}) copy-start(s32[32]{0:T(128)} %occ_s.5) | copy-start | bytes 388
  9.5 22.7 %all-to-all-start.1 = ((f32[8,208,128]{2,1,0:T(8,128)}), f32[8,208,128]{2,1,0:T(8,128)S(1)}, u32[]{:S(2)}, u32[]{:S(2)}) async-start(f32[8,208,128]{2,1,0:T(8,128)} %shard_map.67), calls=%async_computation.2 | async-start | bytes 1703936 | tf_op jit(solution)/shard_map/all_to_all | solution.py:287
  55.2 4.6 %collective-permute-start = (f32[8,304,128]{2,1,0:T(8,128)S(1)}, f32[8,304,128]{2,1,0:T(8,128)S(1)}, u32[]{:S(2)}, u32[]{:S(2)}) collective-permute-start(f32[8,304,128]{2,1,0:T(8,128)S(1)} %all_to_all.34.r2_ref), channel_id=1, source_target_pairs={{0,1},{1,0},{2,3},{3,2},{4,5},{5,4},{6,7},{7,6},{8,9},{9,8},{10,11... | collective-permute-start | bytes 3735560 | tf_op jit(solution)/shard_map/ppermute | solution.py:314
  59.7 2.3 %copy-start.2 = (bf16[384,1024]{1,0:T(8,128)(2,1)}, bf16[384,1024]{1,0:T(8,128)(2,1)S(1)}, u32[]{:S(2)}) copy-start(bf16[384,1024]{1,0:T(8,128)(2,1)S(1)} %shard_map.68.b1_ref) | copy-start | bytes 2359300
  62.1 0.7 copy-start
  62.8 12.1 %all-to-all-start.3 = ((f32[8,32,128]{2,1,0:T(8,128)}), f32[8,32,128]{2,1,0:T(8,128)S(1)}, u32[]{:S(2)}, u32[]{:S(2)}) async-start(f32[8,32,128]{2,1,0:T(8,128)} %get-tuple-element.35), calls=%async_computation.4 | async-start | bytes 262144 | tf_op jit(solution)/shard_map/all_to_all | solution.py:287
  66.1 1.1 %copy-start.3 = (bf16[384,1024]{1,0:T(8,128)(2,1)S(1)}, bf16[384,1024]{1,0:T(8,128)(2,1)}, u32[]{:S(2)}) copy-start(bf16[384,1024]{1,0:T(8,128)(2,1)} %copy-done.2) | copy-start | bytes 2359300
  74.8 20.6 %copy-start.1 = (f32[512,128]{1,0:T(8,128)S(1)}, f32[512,128]{1,0:T(8,128)}, u32[]{:S(2)}) copy-start(f32[512,128]{1,0:T(8,128)} %copy-done) | copy-start | bytes 786436
  74.8 22.4 %copy-start.5 = (f32[96,8,128]{2,1,0:T(8,128)S(1)}, f32[96,8,128]{2,1,0:T(8,128)}, u32[]{:S(2)}) copy-start(f32[96,8,128]{2,1,0:T(8,128)} %b_ref.1) | copy-start | bytes 1179652
  74.8 22.4 %copy-start.7 = (f32[4,4,8,128]{3,2,1,0:T(8,128)S(1)}, f32[4,4,8,128]{3,2,1,0:T(8,128)}, u32[]{:S(2)}) copy-start(f32[4,4,8,128]{3,2,1,0:T(8,128)} %t_ref.5) | copy-start | bytes 196612
  74.8 22.4 %copy-start.12 = (f32[768,4,8]{0,2,1:T(8,128)S(1)}, f32[768,4,8]{0,2,1:T(8,128)}, u32[]{:S(2)}) copy-start(f32[768,4,8]{0,2,1:T(8,128)} %param.10) | copy-start | bytes 294916
  75.7 19.7 %all-to-all-start.4 = ((f32[8,160,128]{2,1,0:T(8,128)}), f32[8,160,128]{2,1,0:T(8,128)S(1)}, u32[]{:S(2)}, u32[]{:S(2)}) async-start(f32[8,160,128]{2,1,0:T(8,128)} %shard_map.72), calls=%async_computation.5 | async-start | bytes 1310720 | tf_op jit(solution)/shard_map/all_to_all | solution.py:287

commit v3 on v2

--- a/solution.py
+++ b/solution.py
@@ -46,14 +46,14 @@
     return lax.dot_general(x, y, (((1,), (1,)), ((), ())), precision=precision, preferred_element_type=F32)
 
 
-def call(body, outs, n_smem, n_vmem, scratch=(), cost=(0, 0)):
+def call(body, outs, n_smem, n_vmem, scratch=(), cost=(0, 0), limit=LIMIT):
     return pl.pallas_call(
         body,
         out_shape=outs,
         in_specs=[SMEM] * n_smem + [VMEM] * n_vmem,
         out_specs=jax.tree.map(lambda _: VMEM, outs),
         scratch_shapes=list(scratch),
-        compiler_params=pltpu.CompilerParams(vmem_limit_bytes=LIMIT),
+        compiler_params=pltpu.CompilerParams(vmem_limit_bytes=limit),
         cost_estimate=pl.CostEstimate(flops=cost[0], bytes_accessed=cost[1], transcendentals=0),
     )
 
@@ -251,7 +251,7 @@
         acc_ref[...] += r[:, :128] + r[:, 128:] + dot(lo_ref[...], hi)
         return carry
 
-    lax.fori_loop(0, 8, step, 0)
+    lax.fori_loop(0, 8, step, 0, unroll=True)
     for a in range(8):
         rows = jnp.transpose(acc_ref[a * 128 : a * 128 + 128, :])
         for p in range(8):
@@ -292,7 +292,7 @@
     shape = jax.ShapeDtypeStruct
     p1 = call(
         fold_local, shape((8, 8 * SL + 16, 128), F32), 1, 4, [pltpu.VMEM((8, 16, 8, 128), F32)],
-        (2 * 2 * 24 * 96 * 1024, 1300000),
+        (2 * 2 * 24 * 96 * 1024, 1300000), 56 * 2**20,
     )(vir, aux, row, b, t)
     r1 = swap(p1, OCC)
     ch, sw, fits = pl.pallas_call(
@@ -339,23 +339,29 @@
     return (jnp.bitwise_xor(left, right) == target).astype(F32)
 
 
+def gather(x, axes, n, dim):
+    parts = swap(jnp.broadcast_to(x[None], (n,) + x.shape), axes)
+    return jnp.concatenate([parts[p] for p in range(n)], axis=dim)
+
+
 def dense(t, b, c, occ, vir, aux):
     o, v = occ_at(), vir_at()
     aux_mine = lax.dynamic_slice_in_dim(aux, o * 96, 96)
     vir_mine = lax.dynamic_slice_in_dim(vir, v * 8, 8)
     occ_mine = lax.dynamic_slice_in_dim(occ, o * 4, 4)
     own = b * allowed(vir_mine[None, :, None], vir[None, None, :], aux_mine[:, None, None])
-    wide = lax.all_gather(b, VIR, axis=1, tiled=True)
+    wide = gather(b, VIR, 16, 1)
     wide = wide * allowed(vir[None, :, None], vir[None, None, :], aux_mine[:, None, None])
-    pairs = lax.all_gather(t, OCC, axis=1, tiled=True)
+    pairs = gather(t, OCC, 8, 1)
     inter = jnp.einsum("qac,qbd->acbd", own, wide, precision=HIGHEST)
-    part = jnp.einsum("ijcd,acbd->ijab", lax.all_gather(pairs, VIR, axis=2, tiled=True), inter, precision=HIGHEST)
-    total = lax.psum_scatter(part, OCC, scatter_dimension=1, tiled=True)
+    part = jnp.einsum("ijcd,acbd->ijab", gather(pairs, VIR, 16, 2), inter, precision=HIGHEST)
+    total = jnp.sum(swap(jnp.moveaxis(part.reshape(4, 8, 4, 8, 128), 1, 0), OCC), axis=0)
     swapped = lax.all_to_all(t, VIR, split_axis=3, concat_axis=2, tiled=True)
     u = 2.0 * t - jnp.transpose(swapped, (0, 1, 3, 2))
-    cw = lax.all_gather(c, VIR, axis=2, tiled=True)
+    cw = gather(c, VIR, 16, 2)
     cw = cw * allowed(occ_mine[None, :, None], vir[None, None, :], aux[:, None, None])
-    y = lax.psum(jnp.einsum("ikac,qkc->iaq", u, cw, precision=HIGHEST), OCC)
+    part = jnp.einsum("ikac,qkc->iaq", u, cw, precision=HIGHEST)
+    y = jnp.sum(swap(jnp.broadcast_to(part[None], (8,) + part.shape), OCC), axis=0)
     return total + jnp.einsum("iaq,qjb->ijab", y, cw, precision=HIGHEST)
 
 

time: 105 us -> 91.2 us (0.87)
  between operations: 14.2 us -> 0.73 us
    pallas_call x1, Pallas kernels: 7.49 us -> 5.98 us  [folded(): call(ladder, shape((8, 8, 16, 128), F32), 1, 4, [pltpu.VMEM((16, 16, 8, 1...]
    unnamed x24 -> x16, local copies, waits for them, and re-layouts: 1.89 us -> 2.8 us
  transfers between devices with their start and end apart: 4 -> 4, of which waited for: 3 -> 3; matrix products, arithmetic and copies ran while one was open for 0% -> 0% of each run, Pallas kernels for 11% -> 12%
where the time goes in v3:
time: 91.2 us; the launch traced here: 90.6 us
  waiting for transfers between devices  25.8 us (28%)
  blocking collectives  21.7 us (24%)
  Pallas kernels  20.2 us (22%)
  starting transfers between devices  19.5 us (21%)
  local copies, waits for them, and re-layouts  2.8 us (3%)
    all_to_all x3, waiting for transfers between devices, swap(): return lax.all_to_all(x, axes, 0, 0, tiled=True)  25.6 us
    all_to_all x1, blocking collectives, swap(): return lax.all_to_all(x, axes, 0, 0, tiled=True)  21.7 us
    all_to_all x3, starting transfers between devices, swap(): return lax.all_to_all(x, axes, 0, 0, tiled=True)  17.4 us
    pallas_call x1, Pallas kernels, folded(): call(ladder, shape((8, 8, 16, 128), F32), 1, 4, [pltpu.VMEM((16, 16, 8, 1...  5.98 us
    pallas_call x1, Pallas kernels, folded(): call(fold_local, shape((8, 8 * SL + 16, 128), F32), 1, 4, [pltpu.VMEM((8,...  2.93 us
    unnamed x16, local copies, waits for them, and re-layouts  2.8 us
    pallas_call x1, Pallas kernels, folded(): call(cycle_first, (shape((8, 32, 128), F32), shape((512, 128), F32)), 1,...  2.55 us
    pallas_call x1, Pallas kernels, folded(): call(refold_rows, shape((384, 1024), BF16), 1, 3, [pltpu.VMEM((2048, 128)...  2.4 us
  transfers between devices with their start and end apart: 4, of which 3 were waited for; matrix products, arithmetic and copies ran while one was open for 0% of the time, Pallas kernels for 12%

profile of v3, /device:TPU:1, one launch (start us, length us, event | category | flops | bytes accessed | tf_op | source)
XLA Modules:
  0.0 90.6 jit_solution(11156132955928793895)
XLA Ops:
  0.0 2.9 %shard_map.67 = f32[8,208,128]{2,1,0:T(8,128)} custom-call(s32[128]{0:T(128)} %vir_s.9, s32[6,128]{1,0:T(8,128)} %bitcast.285, s32[1,128]{1,0:T(1,128)} %bitcast.289, f32[96,8,128]{2,1,0:T(8,128)} %b_ref.1, f32[4,4,8,128]{3,2,1,0:T(8,128)} %t_ref.5), custom_call_target="tpu_custom_call" | custom-call | flops 9437184 | bytes 1300000 | tf_op jit(solution)/shard_map/pallas_call | solution.py:293
  2.9 7.5 %all-to-all-start.7 = ((f32[8,208,128]{2,1,0:T(8,128)}), f32[8,208,128]{2,1,0:T(8,128)S(1)}, u32[]{:S(2)}, u32[]{:S(2)}) async-start(f32[8,208,128]{2,1,0:T(8,128)} %shard_map.67), calls=%async_computation.7 | async-start | bytes 1703936 | tf_op jit(solution)/shard_map/all_to_all | solution.py:287
  10.4 2.1 %shard_map.66 = (f32[32,128]{1,0:T(8,128)S(1)}, f32[128,128]{1,0:T(8,128)S(1)}, s32[1]{0:T(128)}) custom-call(s32[128]{0:T(128)} %vir_s.9, s32[32]{0:T(128)} %occ_s.5, s32[6,128]{1,0:T(8,128)} %bitcast.286, f32[4,8,768]{2,1,0:T(8,128)} %bitcast.284, f32[4,4,8,128]{3,2,1,0:T(8,128)} %t_ref.5), custom_call_target="tpu_custom_call" | custom-call | flops 9437184 | bytes 300000 | tf_op jit(solution)/shard_map/pallas_call | solution.py:298
  12.5 13.1 %all-to-all-done.7.r1_ref = f32[8,208,128]{2,1,0:T(8,128)S(1)} async-done(((f32[8,208,128]{2,1,0:T(8,128)}), f32[8,208,128]{2,1,0:T(8,128)S(1)}, u32[]{:S(2)}, u32[]{:S(2)}) %all-to-all-start.7) | async-done | bytes 852000 | tf_op jit(solution)/shard_map/all_to_all | solution.py:287
  25.6 1.6 %shard_map.69 = f32[8,304,128]{2,1,0:T(8,128)S(1)} custom-call(s32[128]{0:T(128)} %vir_s.9, s32[6,128]{1,0:T(8,128)} %bitcast.287, s32[1,128]{1,0:T(1,128)} %bitcast.290, f32[8,208,128]{2,1,0:T(8,128)S(1)} %all-to-all-done.7.r1_ref, f32[32,128]{1,0:T(8,128)S(1)} %get-tuple-element.33.ch_ref, f32[128,128]{1,0:T(8,128)S(1)} %get-tuple-element.34.sw_ref), custom_call_target="tpu_custom_call" | custom-call | flops 134217728 | bytes 2300000 | tf_op jit(solution)/shard_map/pallas_call | solution.py:306
  27.2 21.7 %all_to_all.59.r2_ref = f32[8,304,128]{2,1,0:T(8,128)S(1)} all-to-all(f32[8,304,128]{2,1,0:T(8,128)S(1)} %shard_map.69), channel_id=1, replica_groups=mesh['yh'=2,'x'=4,'z'=4,'yl'=2,'core'=2] {'z','yl'}, dimensions={0} | all-to-all | bytes 2490368 | tf_op jit(solution)/shard_map/all_to_all | solution.py:287
  48.9 2.1 %collective-permute-start = (f32[8,304,128]{2,1,0:T(8,128)S(1)}, f32[8,304,128]{2,1,0:T(8,128)S(1)}, u32[]{:S(2)}, u32[]{:S(2)}) collective-permute-start(f32[8,304,128]{2,1,0:T(8,128)S(1)} %all_to_all.59.r2_ref), channel_id=1, source_target_pairs={{0,1},{1,0},{2,3},{3,2},{4,5},{5,4},{6,7},{7,6},{8,9},{9,8},{10,11... | collective-permute-start | bytes 3735560 | tf_op jit(solution)/shard_map/ppermute | solution.py:314
  50.9 0.0 copy-done.8
  50.9 0.0 copy-done.7
  50.9 2.4 %shard_map.68.b1_ref = bf16[384,1024]{1,0:T(8,128)(2,1)S(1)} custom-call(s32[128]{0:T(128)S(1)} %copy-done.8, s32[6,128]{1,0:T(8,128)S(1)} %bitcast.288, s32[1,128]{1,0:T(1,128)S(1)} %bitcast.291, f32[8,208,128]{2,1,0:T(8,128)S(1)} %all-to-all-done.7.r1_ref), custom_call_target="tpu_custom_call" | custom-call | flops 1073741824 | bytes 1700000 | tf_op jit(solution)/shard_map/pallas_call | solution.py:311
  53.4 0.0 copy-start.2
  53.4 0.1 collective-permute-done.o2_ref
  53.5 2.5 %shard_map.71 = (f32[8,32,128]{2,1,0:T(8,128)}, f32[512,128]{1,0:T(8,128)S(1)}) custom-call(s32[32]{0:T(128)S(1)} %copy-done.10, s32[1,128]{1,0:T(1,128)S(1)} %bitcast.292, f32[8,304,128]{2,1,0:T(8,128)S(1)} %all_to_all.59.r2_ref, f32[8,304,128]{2,1,0:T(8,128)S(1)} %collective-permute-done.o2_ref, f32[4,4,8,128]{3,2,1,0:T(8,128)} %t_ref.5), custom_call_target="tpu_custom_call" | custom-call | flops 201326592 | bytes 4000000 | tf_op jit(solution)/shard_map/pallas_call | solution.py:315
  56.1 0.7 copy-done
  56.8 3.4 %all-to-all-start.9 = ((f32[8,32,128]{2,1,0:T(8,128)}), f32[8,32,128]{2,1,0:T(8,128)S(1)}, u32[]{:S(2)}, u32[]{:S(2)}) async-start(f32[8,32,128]{2,1,0:T(8,128)} %get-tuple-element.35), calls=%async_computation.9 | async-start | bytes 262144 | tf_op jit(solution)/shard_map/all_to_all | solution.py:287
  60.2 0.0 copy-start.3
  60.2 1.1 %copy-done.3 = bf16[384,1024]{1,0:T(8,128)(2,1)S(1)} copy-done((bf16[384,1024]{1,0:T(8,128)(2,1)S(1)}, bf16[384,1024]{1,0:T(8,128)(2,1)}, u32[]{:S(2)}) %copy-start.3) | copy-done | bytes 786456
  61.3 6.0 %shard_map.70.p3_ref = f32[8,8,16,128]{3,2,1,0:T(8,128)S(1)} custom-call(s32[128]{0:T(128)S(1)} %copy-done.8, s32[1,128]{1,0:T(1,128)S(1)} %bitcast.293, bf16[384,1024]{1,0:T(8,128)(2,1)S(1)} %copy-done.3, f32[8,304,128]{2,1,0:T(8,128)S(1)} %all_to_all.59.r2_ref, f32[8,304,128]{2,1,0:T(8,128)S(1)} %collective-permute-done.o2_ref), custom_call_target="tpu_custom_call" | custom-call | flops 3221225472 | bytes 4000000 | tf_op jit(solution)/shard_map/pallas_call | solution.py:320
  67.3 0.0 all-to-all-done.9.y_ref
  67.3 0.9 %shard_map.72 = f32[8,160,128]{2,1,0:T(8,128)} custom-call(f32[8,8,16,128]{3,2,1,0:T(8,128)S(1)} %shard_map.70.p3_ref, f32[8,32,128]{2,1,0:T(8,128)S(1)} %all-to-all-done.9.y_ref), custom_call_target="tpu_custom_call" | custom-call | bytes 1300000 | tf_op jit(solution)/shard_map/pallas_call | solution.py:331
  68.2 6.6 %all-to-all-start.10 = ((f32[8,160,128]{2,1,0:T(8,128)}), f32[8,160,128]{2,1,0:T(8,128)S(1)}, u32[]{:S(2)}, u32[]{:S(2)}) async-start(f32[8,160,128]{2,1,0:T(8,128)} %shard_map.72), calls=%async_computation.10 | async-start | bytes 1310720 | tf_op jit(solution)/shard_map/all_to_all | solution.py:287
  75.4 12.5 %all-to-all-done.10.r3_ref = f32[8,160,128]{2,1,0:T(8,128)S(1)} async-done(((f32[8,160,128]{2,1,0:T(8,128)}), f32[8,160,128]{2,1,0:T(8,128)S(1)}, u32[]{:S(2)}, u32[]{:S(2)}) %all-to-all-start.10) | async-done | bytes 655392 | tf_op jit(solution)/shard_map/all_to_all | solution.py:287
  87.9 0.9 %copy-done.1 = f32[512,128]{1,0:T(8,128)S(1)} copy-done((f32[512,128]{1,0:T(8,128)S(1)}, f32[512,128]{1,0:T(8,128)}, u32[]{:S(2)}) %copy-start.1) | copy-done | bytes 262168
  88.8 1.8 %shard_map.73 = f32[4,4,8,128]{3,2,1,0:T(8,128)} custom-call(s32[32]{0:T(128)S(1)} %copy-done.10, s32[1,128]{1,0:T(1,128)S(1)} %bitcast.294, f32[8,160,128]{2,1,0:T(8,128)S(1)} %all-to-all-done.10.r3_ref, f32[512,128]{1,0:T(8,128)S(1)} %copy-done.1), custom_call_target="tpu_custom_call" | custom-call | flops 201326592 | bytes 2000000 | tf_op jit(solution)/shard_map/pallas_call | solution.py:332
  (10 shorter events, 0.0 us)
Async XLA Ops:
  0.0 50.9 %copy-start.8 = (s32[128]{0:T(128)S(1)}, s32[128]{0:T(128)}, u32[]{:S(2)}) copy-start(s32[128]{0:T(128)} %vir_s.9) | copy-start | bytes 1540
  0.0 50.9 %copy-start.7 = (s32[768]{0:T(1024)S(1)}, s32[768]{0:T(1024)}, u32[]{:S(2)}) copy-start(s32[768]{0:T(1024)} %param.13) | copy-start | bytes 9220
  0.0 53.5 %copy-start.10 = (s32[32]{0:T(128)S(1)}, s32[32]{0:T(128)}, u32[]{:S(2)}) copy-start(s32[32]{0:T(128)} %occ_s.5) | copy-start | bytes 388
  2.9 22.7 %all-to-all-start.7 = ((f32[8,208,128]{2,1,0:T(8,128)}), f32[8,208,128]{2,1,0:T(8,128)S(1)}, u32[]{:S(2)}, u32[]{:S(2)}) async-start(f32[8,208,128]{2,1,0:T(8,128)} %shard_map.67), calls=%async_computation.7 | async-start | bytes 1703936 | tf_op jit(solution)/shard_map/all_to_all | solution.py:287
  48.9 4.6 %collective-permute-start = (f32[8,304,128]{2,1,0:T(8,128)S(1)}, f32[8,304,128]{2,1,0:T(8,128)S(1)}, u32[]{:S(2)}, u32[]{:S(2)}) collective-permute-start(f32[8,304,128]{2,1,0:T(8,128)S(1)} %all_to_all.59.r2_ref), channel_id=1, source_target_pairs={{0,1},{1,0},{2,3},{3,2},{4,5},{5,4},{6,7},{7,6},{8,9},{9,8},{10,11... | collective-permute-start | bytes 3735560 | tf_op jit(solution)/shard_map/ppermute | solution.py:314
  53.4 2.7 %copy-start.2 = (bf16[384,1024]{1,0:T(8,128)(2,1)}, bf16[384,1024]{1,0:T(8,128)(2,1)S(1)}, u32[]{:S(2)}) copy-start(bf16[384,1024]{1,0:T(8,128)(2,1)S(1)} %shard_map.68.b1_ref) | copy-start | bytes 2359300
  56.1 0.7 copy-start
  56.8 10.5 %all-to-all-start.9 = ((f32[8,32,128]{2,1,0:T(8,128)}), f32[8,32,128]{2,1,0:T(8,128)S(1)}, u32[]{:S(2)}, u32[]{:S(2)}) async-start(f32[8,32,128]{2,1,0:T(8,128)} %get-tuple-element.35), calls=%async_computation.9 | async-start | bytes 262144 | tf_op jit(solution)/shard_map/all_to_all | solution.py:287
  60.2 1.1 %copy-start.3 = (bf16[384,1024]{1,0:T(8,128)(2,1)S(1)}, bf16[384,1024]{1,0:T(8,128)(2,1)}, u32[]{:S(2)}) copy-start(bf16[384,1024]{1,0:T(8,128)(2,1)} %copy-done.2) | copy-start | bytes 2359300
  61.3 29.3 %copy-start.6 = (f32[768,4,8]{0,2,1:T(8,128)S(1)}, f32[768,4,8]{0,2,1:T(8,128)}, u32[]{:S(2)}) copy-start(f32[768,4,8]{0,2,1:T(8,128)} %param.10) | copy-start | bytes 294916
  68.2 19.7 %all-to-all-start.10 = ((f32[8,160,128]{2,1,0:T(8,128)}), f32[8,160,128]{2,1,0:T(8,128)S(1)}, u32[]{:S(2)}, u32[]{:S(2)}) async-start(f32[8,160,128]{2,1,0:T(8,128)} %shard_map.72), calls=%async_computation.10 | async-start | bytes 1310720 | tf_op jit(solution)/shard_map/all_to_all | solution.py:287
  87.9 1.0 %copy-start.1 = (f32[512,128]{1,0:T(8,128)S(1)}, f32[512,128]{1,0:T(8,128)}, u32[]{:S(2)}) copy-start(f32[512,128]{1,0:T(8,128)} %copy-done) | copy-start | bytes 786436

commit v4 on v3

--- a/solution.py
+++ b/solution.py
@@ -190,14 +190,15 @@
             keep = (label == g).astype(F32)
             keep = jnp.concatenate([keep, keep], axis=1).astype(BF16)
             total = total + dot(spread[:, g * 256 : (g + 1) * 256], both * keep)
-        hi, lo = split(total[:, :128] + total[:, 128:])
-        out_ref[0:128, x * 128 : x * 128 + 128] = hi
-        out_ref[128:256, x * 128 : x * 128 + 128] = lo
-        out_ref[256:384, x * 128 : x * 128 + 128] = hi
-
-
-def cycle_first(occ_s, vir_ref, r2_ref, o2_ref, t_ref, y_ref, chat_ref, got_ref):
+        out_ref[:, x * 128 : x * 128 + 128] = total[:, :128] + total[:, 128:]
+
+
+def cycle_first(occ_s, vir_ref, r2_ref, o2_ref, t_ref, b1_ref, y_ref, chat_ref, cat_ref, f_ref, amps_ref, got_ref):
     o, core = occ_at(), lax.axis_index("core")
+    for ref, part in ((r2_ref, core), (o2_ref, 1 - core)):
+        for p in range(8):
+            f_ref[:, 2 * p + part] = ref[p, 0:128, :].reshape(16, 8, 128)
+            amps_ref[:, 2 * p + part] = ref[p, 128:256, :].reshape(16, 8, 128)
     for p in range(8):
         got_ref[2 * p + core] = r2_ref[p, 256:304, :]
         got_ref[2 * p + 1 - core] = o2_ref[p, 256:304, :]
@@ -219,16 +220,14 @@
     u = jnp.concatenate(u, axis=0)
     label = jnp.concatenate([vir_ref[...] ^ occ_s[o * 4 + k] for k in range(4)], axis=1)
     rows = jnp.concatenate([jnp.where(label == g, u, 0.0) for g in range(NG)], axis=0)
-    y = jnp.dot(rows, chat_ref[...], precision=HIGHEST, preferred_element_type=F32)
+    y = jnp.dot(rows, chat_ref[...], precision=lax.Precision.HIGH, preferred_element_type=F32)
     y_ref[...] = y.reshape(8, 32, 128)
-
-
-def ladder(vir_s, vir_ref, b1_ref, r2_ref, o2_ref, out_ref, f_ref, t_ref, hi_ref, lo_ref, acc_ref):
-    o, v, core = occ_at(), vir_at(), lax.axis_index("core")
-    for ref, part in ((r2_ref, core), (o2_ref, 1 - core)):
-        for p in range(8):
-            f_ref[:, 2 * p + part] = ref[p, 0:128, :].reshape(16, 8, 128)
-            t_ref[:, 2 * p + part] = ref[p, 128:256, :].reshape(16, 8, 128)
+    hi, lo = split(b1_ref[...])
+    cat_ref[0:128], cat_ref[128:256], cat_ref[256:384] = hi, lo, hi
+
+
+def ladder(vir_s, vir_ref, b1_ref, f_ref, t_ref, _, acc_ref, hi_ref, lo_ref):
+    o, v = occ_at(), vir_at()
     acc_ref[...] = jnp.zeros_like(acc_ref)
     c_lane = jnp.broadcast_to(vir_ref[...], (128, 128))
     bc = jnp.transpose(c_lane) ^ c_lane
@@ -252,18 +251,17 @@
         return carry
 
     lax.fori_loop(0, 8, step, 0, unroll=True)
-    for a in range(8):
-        rows = jnp.transpose(acc_ref[a * 128 : a * 128 + 128, :])
-        for p in range(8):
-            out_ref[p, a] = rows[16 * p : 16 * p + 16, :]
-
-
-def join(p3_ref, y_ref, out_ref):
+
+
+def join(p3_ref, y_ref, _, out_ref):
     y = y_ref[0]
     for p in range(1, 8):
         y = y + y_ref[p]
+    for a in range(8):
+        rows = jnp.transpose(p3_ref[a * 128 : a * 128 + 128, :])
+        for p in range(8):
+            out_ref[p, 16 * a : 16 * a + 16, :] = rows[16 * p : 16 * p + 16, :]
     for p in range(8):
-        out_ref[p, 0:128, :] = p3_ref[p].reshape(128, 128)
         out_ref[p, 128:160, :] = y
 
 
@@ -273,7 +271,7 @@
     for p in range(1, 8):
         total = total + r3_ref[p, 0:128, :]
     sum_ref[...] = total
-    z = dot_t(jnp.concatenate([r3_ref[p, 128:160, :] for p in range(8)], axis=0), chat_ref[...], HIGHEST)
+    z = dot_t(jnp.concatenate([r3_ref[p, 128:160, :] for p in range(8)], axis=0), chat_ref[...], lax.Precision.HIGH)
     for j in range(4):
         label = vir_ref[...] ^ occ_s[o * 4 + j]
         part = jnp.zeros((32, 128), F32)
@@ -309,26 +307,25 @@
     )(vir, aux, row, r1, ch, sw)
     r2 = swap(p2, ZY)
     b1 = call(
-        refold_rows, shape((384, 1024), BF16), 1, 3, [pltpu.VMEM((2048, 128), F32)], (2 * 128 * 2048 * 2048, 1700000)
+        refold_rows, shape((SG, 1024), F32), 1, 3, [pltpu.VMEM((2048, 128), F32)], (2 * 128 * 2048 * 2048, 1700000)
     )(vir, aux, row, r1)
     o2 = lax.ppermute(r2, "core", [(0, 1), (1, 0)])
-    yp, chat = call(
-        cycle_first, (shape((8, 32, 128), F32), shape((512, 128), F32)), 1, 4, [pltpu.VMEM((16, 48, 128), F32)],
+    staged = shape((16, 16, 8, 128), F32)
+    yp, chat, cat, f, amps = call(
+        cycle_first, (shape((8, 32, 128), F32), shape((512, 128), F32), shape((384, 1024), BF16), staged, staged), 1, 5,
+        [pltpu.VMEM((16, 48, 128), F32)],
         (6 * 2 * 256 * 512 * 128, 4000000),
-    )(occ, row, r2, o2, t)
+    )(occ, row, r2, o2, t, b1)
     yr = swap(yp, OCC)
     p3 = call(
-        ladder, shape((8, 8, 16, 128), F32), 1, 4,
+        ladder, shape((1024, 128), F32), 1, 5,
         [
-            pltpu.VMEM((16, 16, 8, 128), F32),
-            pltpu.VMEM((16, 16, 8, 128), F32),
             pltpu.VMEM((1024, 256), BF16),
             pltpu.VMEM((1024, 256), BF16),
-            pltpu.VMEM((1024, 128), F32),
         ],
         (6 * 2048 * 1024 * 256, 4000000),
-    )(vir, row, b1, r2, o2)
-    r3 = swap(call(join, shape((8, 160, 128), F32), 0, 2, (), (0, 1300000))(p3, yr), OCC)
+    )(vir, row, cat, f, amps, chat)
+    r3 = swap(call(join, shape((8, 160, 128), F32), 0, 3, (), (0, 1300000))(p3, yr, chat), OCC)
     out = call(
         finish, shape((4, 4, 8, 128), F32), 1, 3, [pltpu.VMEM((128, 128), F32)], (6 * 2 * 256 * 512 * 128, 2000000)
     )(occ, row, r3, chat)

time: 91.2 us -> 89.6 us (0.982)
    unnamed x16 -> x14, local copies, waits for them, and re-layouts: 2.8 us -> 2.02 us
  transfers between devices with their start and end apart: 4 -> 4, of which waited for: 3 -> 4; matrix products, arithmetic and copies ran while one was open for 0% -> 0% of each run, Pallas kernels for 12% -> 11%
where the time goes in v4:
time: 89.6 us; the launch traced here: 89.1 us
  waiting for transfers between devices  25.8 us (29%)
  blocking collectives  21.7 us (24%)
  Pallas kernels  19.4 us (22%)
  starting transfers between devices  19.4 us (22%)
  local copies, waits for them, and re-layouts  2.02 us (2%)
    all_to_all x3, waiting for transfers between devices, swap(): return lax.all_to_all(x, axes, 0, 0, tiled=True)  25.7 us
    all_to_all x1, blocking collectives, swap(): return lax.all_to_all(x, axes, 0, 0, tiled=True)  21.7 us
    all_to_all x3, starting transfers between devices, swap(): return lax.all_to_all(x, axes, 0, 0, tiled=True)  17.4 us
    pallas_call x1, Pallas kernels, folded(): call(ladder, shape((1024, 128), F32), 1, 5, [pltpu.VMEM((1024, 256), BF16...  5.66 us
    pallas_call x1, Pallas kernels, folded(): call(fold_local, shape((8, 8 * SL + 16, 128), F32), 1, 4, [pltpu.VMEM((8,...  2.93 us
    pallas_call x1, Pallas kernels, folded(): call(refold_rows, shape((SG, 1024), F32), 1, 3, [pltpu.VMEM((2048, 128),...  2.39 us
    pallas_call x1, Pallas kernels, folded(): call(cycle_first, (shape((8, 32, 128), F32), shape((512, 128), F32), shap...  2.22 us
    ppermute x1, starting transfers between devices, folded(): o2 = lax.ppermute(r2, 'core', [(0, 1), (1, 0)])  2.08 us
  transfers between devices with their start and end apart: 4, of which 4 were waited for; matrix products, arithmetic and copies ran while one was open for 0% of the time, Pallas kernels for 11%

profile of v4, /device:TPU:1, one launch (start us, length us, event | category | flops | bytes accessed | tf_op | source)
XLA Modules:
  0.0 89.1 jit_solution(5457422392915525454)
XLA Ops:
  0.0 0.0 copy-start.9
  0.0 2.9 %shard_map.67 = f32[8,208,128]{2,1,0:T(8,128)} custom-call(s32[128]{0:T(128)} %vir_s.9, s32[6,128]{1,0:T(8,128)} %bitcast.285, s32[1,128]{1,0:T(1,128)} %bitcast.289, f32[96,8,128]{2,1,0:T(8,128)} %b_ref.1, f32[4,4,8,128]{3,2,1,0:T(8,128)} %t_ref.5), custom_call_target="tpu_custom_call" | custom-call | flops 9437184 | bytes 1300000 | tf_op jit(solution)/shard_map/pallas_call | solution.py:291
  3.0 7.5 %all-to-all-start.7 = ((f32[8,208,128]{2,1,0:T(8,128)}), f32[8,208,128]{2,1,0:T(8,128)S(1)}, u32[]{:S(2)}, u32[]{:S(2)}) async-start(f32[8,208,128]{2,1,0:T(8,128)} %shard_map.67), calls=%async_computation.7 | async-start | bytes 1703936 | tf_op jit(solution)/shard_map/all_to_all | solution.py:285
  10.4 2.1 %shard_map.66 = (f32[32,128]{1,0:T(8,128)S(1)}, f32[128,128]{1,0:T(8,128)S(1)}, s32[1]{0:T(128)}) custom-call(s32[128]{0:T(128)} %vir_s.9, s32[32]{0:T(128)} %occ_s.5, s32[6,128]{1,0:T(8,128)} %bitcast.286, f32[4,8,768]{2,1,0:T(8,128)} %bitcast.284, f32[4,4,8,128]{3,2,1,0:T(8,128)} %t_ref.5), custom_call_target="tpu_custom_call" | custom-call | flops 9437184 | bytes 300000 | tf_op jit(solution)/shard_map/pallas_call | solution.py:296
  12.5 13.1 %all-to-all-done.7.r1_ref = f32[8,208,128]{2,1,0:T(8,128)S(1)} async-done(((f32[8,208,128]{2,1,0:T(8,128)}), f32[8,208,128]{2,1,0:T(8,128)S(1)}, u32[]{:S(2)}, u32[]{:S(2)}) %all-to-all-start.7) | async-done | bytes 852000 | tf_op jit(solution)/shard_map/all_to_all | solution.py:285
  25.6 1.6 %shard_map.68 = f32[8,304,128]{2,1,0:T(8,128)S(1)} custom-call(s32[128]{0:T(128)} %vir_s.9, s32[6,128]{1,0:T(8,128)} %bitcast.287, s32[1,128]{1,0:T(1,128)} %bitcast.290, f32[8,208,128]{2,1,0:T(8,128)S(1)} %all-to-all-done.7.r1_ref, f32[32,128]{1,0:T(8,128)S(1)} %get-tuple-element.36.ch_ref, f32[128,128]{1,0:T(8,128)S(1)} %get-tuple-element.37.sw_ref), custom_call_target="tpu_custom_call" | custom-call | flops 134217728 | bytes 2300000 | tf_op jit(solution)/shard_map/pallas_call | solution.py:304
  27.2 21.7 %all_to_all.59.r2_ref = f32[8,304,128]{2,1,0:T(8,128)S(1)} all-to-all(f32[8,304,128]{2,1,0:T(8,128)S(1)} %shard_map.68), channel_id=1, replica_groups=mesh['yh'=2,'x'=4,'z'=4,'yl'=2,'core'=2] {'z','yl'}, dimensions={0} | all-to-all | bytes 2490368 | tf_op jit(solution)/shard_map/all_to_all | solution.py:285
  48.9 2.1 %collective-permute-start = (f32[8,304,128]{2,1,0:T(8,128)S(1)}, f32[8,304,128]{2,1,0:T(8,128)S(1)}, u32[]{:S(2)}, u32[]{:S(2)}) collective-permute-start(f32[8,304,128]{2,1,0:T(8,128)S(1)} %all_to_all.59.r2_ref), channel_id=1, source_target_pairs={{0,1},{1,0},{2,3},{3,2},{4,5},{5,4},{6,7},{7,6},{8,9},{9,8},{10,11... | collective-permute-start | bytes 3735560 | tf_op jit(solution)/shard_map/ppermute | solution.py:312
  51.0 0.0 copy-done.7
  51.0 0.0 copy-done.6
  51.0 2.4 %shard_map.69.b1_ref = f32[128,1024]{1,0:T(8,128)S(1)} custom-call(s32[128]{0:T(128)S(1)} %copy-done.7, s32[6,128]{1,0:T(8,128)S(1)} %bitcast.288, s32[1,128]{1,0:T(1,128)S(1)} %bitcast.291, f32[8,208,128]{2,1,0:T(8,128)S(1)} %all-to-all-done.7.r1_ref), custom_call_target="tpu_custom_call" | custom-call | flops 1073741824 | bytes 1700000 | tf_op jit(solution)/shard_map/pallas_call | solution.py:309
  53.4 0.2 collective-permute-done.o2_ref
  53.5 0.0 copy-done.3
  53.5 0.0 copy-done.9
  53.5 2.2 %shard_map.70 = (f32[8,32,128]{2,1,0:T(8,128)}, f32[512,128]{1,0:T(8,128)S(1)}, bf16[384,1024]{1,0:T(8,128)(2,1)S(1)}, f32[16,16,8,128]{3,2,1,0:T(8,128)S(1)}, f32[16,16,8,128]{3,2,1,0:T(8,128)S(1)}) custom-call(s32[32]{0:T(128)S(1)} %copy-done.9, s32[1,128]{1,0:T(1,128)S(1)} %bitcast.292, f32[8,304,128]{2,1,0:T(8,128)S(1)} %all_to_all.59.r2_ref, ...), custom_call_target="tpu_custom_call" | custom-call | flops 201326592 | bytes 4000000 | tf_op jit(solution)/shard_map/pallas_call | solution.py:314
  55.8 0.9 copy-done
  56.6 3.4 %all-to-all-start.9 = ((f32[8,32,128]{2,1,0:T(8,128)}), f32[8,32,128]{2,1,0:T(8,128)S(1)}, u32[]{:S(2)}, u32[]{:S(2)}) async-start(f32[8,32,128]{2,1,0:T(8,128)} %get-tuple-element.42), calls=%async_computation.9 | async-start | bytes 262144 | tf_op jit(solution)/shard_map/all_to_all | solution.py:285
  60.0 1.1 %copy-done.1 = bf16[384,1024]{1,0:T(8,128)(2,1)S(1)} copy-done((bf16[384,1024]{1,0:T(8,128)(2,1)S(1)}, bf16[384,1024]{1,0:T(8,128)(2,1)}, u32[]{:S(2)}) %copy-start.1) | copy-done | bytes 786456
  61.1 5.7 %shard_map.71.p3_ref = f32[1024,128]{1,0:T(8,128)S(1)} custom-call(s32[128]{0:T(128)S(1)} %copy-done.7, s32[1,128]{1,0:T(1,128)S(1)} %bitcast.293, bf16[384,1024]{1,0:T(8,128)(2,1)S(1)} %copy-done.1, f32[16,16,8,128]{3,2,1,0:T(8,128)S(1)} %get-tuple-element.39.f_ref, f32[16,16,8,128]{3,2,1,0:T(8,128)S(1)} %get-tuple-element.40.t_ref, ...), custom_call_target="tpu_custom_call" | custom-call | flops 3221225472 | bytes 4000000 | tf_op jit(solution)/shard_map/pallas_call | solution.py:320
  66.8 0.1 all-to-all-done.9.y_ref
  66.9 1.1 %shard_map.72 = f32[8,160,128]{2,1,0:T(8,128)} custom-call(f32[1024,128]{1,0:T(8,128)S(1)} %shard_map.71.p3_ref, f32[8,32,128]{2,1,0:T(8,128)S(1)} %all-to-all-done.9.y_ref, f32[512,128]{1,0:T(8,128)S(1)} %get-tuple-element.41._.chat_ref), custom_call_target="tpu_custom_call" | custom-call | bytes 1300000 | tf_op jit(solution)/shard_map/pallas_call | solution.py:328
  67.9 6.5 %all-to-all-start.10 = ((f32[8,160,128]{2,1,0:T(8,128)}), f32[8,160,128]{2,1,0:T(8,128)S(1)}, u32[]{:S(2)}, u32[]{:S(2)}) async-start(f32[8,160,128]{2,1,0:T(8,128)} %shard_map.72), calls=%async_computation.10 | async-start | bytes 1310720 | tf_op jit(solution)/shard_map/all_to_all | solution.py:285
  75.1 12.5 %all-to-all-done.10.r3_ref = f32[8,160,128]{2,1,0:T(8,128)S(1)} async-done(((f32[8,160,128]{2,1,0:T(8,128)}), f32[8,160,128]{2,1,0:T(8,128)S(1)}, u32[]{:S(2)}, u32[]{:S(2)}) %all-to-all-start.10) | async-done | bytes 655392 | tf_op jit(solution)/shard_map/all_to_all | solution.py:285
  87.6 1.5 %shard_map.73 = f32[4,4,8,128]{3,2,1,0:T(8,128)} custom-call(s32[32]{0:T(128)S(1)} %copy-done.9, s32[1,128]{1,0:T(1,128)S(1)} %bitcast.294, f32[8,160,128]{2,1,0:T(8,128)S(1)} %all-to-all-done.10.r3_ref, f32[512,128]{1,0:T(8,128)S(1)} %get-tuple-element.41._.chat_ref), custom_call_target="tpu_custom_call" | custom-call | flops 201326592 | bytes 2000000 | tf_op jit(solution)/shard_map/pallas_call | solution.py:329
  (8 shorter events, 0.0 us)
Async XLA Ops:
  0.0 51.0 %copy-start.7 = (s32[128]{0:T(128)S(1)}, s32[128]{0:T(128)}, u32[]{:S(2)}) copy-start(s32[128]{0:T(128)} %vir_s.9) | copy-start | bytes 1540
  0.0 51.0 %copy-start.6 = (s32[768]{0:T(1024)S(1)}, s32[768]{0:T(1024)}, u32[]{:S(2)}) copy-start(s32[768]{0:T(1024)} %param.13) | copy-start | bytes 9220
  0.0 53.5 %copy-start.3 = (f32[4,4,8,128]{3,2,1,0:T(8,128)S(1)}, f32[4,4,8,128]{3,2,1,0:T(8,128)}, u32[]{:S(2)}) copy-start(f32[4,4,8,128]{3,2,1,0:T(8,128)} %t_ref.5) | copy-start | bytes 196612
  0.0 53.5 %copy-start.9 = (s32[32]{0:T(128)S(1)}, s32[32]{0:T(128)}, u32[]{:S(2)}) copy-start(s32[32]{0:T(128)} %occ_s.5) | copy-start | bytes 388
  3.0 22.7 %all-to-all-start.7 = ((f32[8,208,128]{2,1,0:T(8,128)}), f32[8,208,128]{2,1,0:T(8,128)S(1)}, u32[]{:S(2)}, u32[]{:S(2)}) async-start(f32[8,208,128]{2,1,0:T(8,128)} %shard_map.67), calls=%async_computation.7 | async-start | bytes 1703936 | tf_op jit(solution)/shard_map/all_to_all | solution.py:285
  48.9 4.6 %collective-permute-start = (f32[8,304,128]{2,1,0:T(8,128)S(1)}, f32[8,304,128]{2,1,0:T(8,128)S(1)}, u32[]{:S(2)}, u32[]{:S(2)}) collective-permute-start(f32[8,304,128]{2,1,0:T(8,128)S(1)} %all_to_all.59.r2_ref), channel_id=1, source_target_pairs={{0,1},{1,0},{2,3},{3,2},{4,5},{5,4},{6,7},{7,6},{8,9},{9,8},{10,11... | collective-permute-start | bytes 3735560 | tf_op jit(solution)/shard_map/ppermute | solution.py:312
  55.8 0.9 copy-start
  56.6 10.3 %all-to-all-start.9 = ((f32[8,32,128]{2,1,0:T(8,128)}), f32[8,32,128]{2,1,0:T(8,128)S(1)}, u32[]{:S(2)}, u32[]{:S(2)}) async-start(f32[8,32,128]{2,1,0:T(8,128)} %get-tuple-element.42), calls=%async_computation.9 | async-start | bytes 262144 | tf_op jit(solution)/shard_map/all_to_all | solution.py:285
  60.0 1.1 %copy-start.1 = (bf16[384,1024]{1,0:T(8,128)(2,1)S(1)}, bf16[384,1024]{1,0:T(8,128)(2,1)}, u32[]{:S(2)}) copy-start(bf16[384,1024]{1,0:T(8,128)(2,1)} %copy-done) | copy-start | bytes 2359300
  61.1 28.0 %copy-start.2 = (f32[96,8,128]{2,1,0:T(8,128)S(1)}, f32[96,8,128]{2,1,0:T(8,128)}, u32[]{:S(2)}) copy-start(f32[96,8,128]{2,1,0:T(8,128)} %b_ref.1) | copy-start | bytes 1179652
  67.9 19.6 %all-to-all-start.10 = ((f32[8,160,128]{2,1,0:T(8,128)}), f32[8,160,128]{2,1,0:T(8,128)S(1)}, u32[]{:S(2)}, u32[]{:S(2)}) async-start(f32[8,160,128]{2,1,0:T(8,128)} %shard_map.72), calls=%async_computation.10 | async-start | bytes 1310720 | tf_op jit(solution)/shard_map/all_to_all | solution.py:285

commit v5 on v4

--- a/solution.py
+++ b/solution.py
@@ -42,8 +42,13 @@
     return jnp.dot(x, y, preferred_element_type=F32)
 
 
-def dot_t(x, y, precision=None):
-    return lax.dot_general(x, y, (((1,), (1,)), ((), ())), precision=precision, preferred_element_type=F32)
+def dot_t(x, y):
+    return lax.dot_general(x, y, (((1,), (1,)), ((), ())), preferred_element_type=F32)
+
+
+def dot3(x, y, product):
+    (xh, xl), (yh, yl) = split(x), split(y)
+    return product(xh, yh) + product(xh, yl) + product(xl, yh)
 
 
 def call(body, outs, n_smem, n_vmem, scratch=(), cost=(0, 0), limit=LIMIT):
@@ -100,7 +105,7 @@
         out_ref[peer, 8 * SL : 8 * SL + 16, :] = block
 
 
-def fold_ov(vir_s, occ_s, aux_ref, c_ref, t_ref, ch_ref, sw_ref, fits_ref):
+def fold_ov(vir_s, occ_s, aux_ref, c_ref, t_ref, ch_ref, sw_ref, pick_ref, fits_ref):
     o, v = occ_at(), vir_at()
     rows = aux_blocks(aux_ref)
     over = jnp.zeros((8, 1), F32)
@@ -113,6 +118,7 @@
     before = (iota((768, 768), 0) < iota((768, 768), 1)).astype(F32).astype(BF16)
     rank = jnp.sum(member * dot(member.astype(BF16), before), axis=0, keepdims=True)
     pick = (rank == iota((SG, 768), 0).astype(F32)).astype(F32).astype(BF16)
+    pick_ref[...] = pick
     c_label = jnp.zeros((8, 1), jnp.int32)
     for c in range(8):
         c_label = jnp.where(iota((8, 1), 0) == c, vir_s[v * 8 + c], c_label)
@@ -190,10 +196,13 @@
             keep = (label == g).astype(F32)
             keep = jnp.concatenate([keep, keep], axis=1).astype(BF16)
             total = total + dot(spread[:, g * 256 : (g + 1) * 256], both * keep)
-        out_ref[:, x * 128 : x * 128 + 128] = total[:, :128] + total[:, 128:]
-
-
-def cycle_first(occ_s, vir_ref, r2_ref, o2_ref, t_ref, b1_ref, y_ref, chat_ref, cat_ref, f_ref, amps_ref, got_ref):
+        hi, lo = split(total[:, :128] + total[:, 128:])
+        out_ref[0:128, x * 128 : x * 128 + 128] = hi
+        out_ref[128:256, x * 128 : x * 128 + 128] = lo
+        out_ref[256:384, x * 128 : x * 128 + 128] = hi
+
+
+def cycle_first(occ_s, vir_ref, r2_ref, o2_ref, t_ref, pick_ref, aux_ref, y_ref, chat_ref, f_ref, amps_ref, got_ref):
     o, core = occ_at(), lax.axis_index("core")
     for ref, part in ((r2_ref, core), (o2_ref, 1 - core)):
         for p in range(8):
@@ -220,13 +229,17 @@
     u = jnp.concatenate(u, axis=0)
     label = jnp.concatenate([vir_ref[...] ^ occ_s[o * 4 + k] for k in range(4)], axis=1)
     rows = jnp.concatenate([jnp.where(label == g, u, 0.0) for g in range(NG)], axis=0)
-    y = jnp.dot(rows, chat_ref[...], precision=lax.Precision.HIGH, preferred_element_type=F32)
-    y_ref[...] = y.reshape(8, 32, 128)
-    hi, lo = split(b1_ref[...])
-    cat_ref[0:128], cat_ref[128:256], cat_ref[256:384] = hi, lo, hi
-
-
-def ladder(vir_s, vir_ref, b1_ref, f_ref, t_ref, _, acc_ref, hi_ref, lo_ref):
+    hi, lo = split(dot3(rows, chat_ref[...], dot))
+    y = dot(hi, pick_ref[...]) + dot(lo, pick_ref[...])
+    for n in range(6):
+        aux = aux_ref[n : n + 1, :]
+        part = jnp.zeros((32, 128), F32)
+        for g in range(NG):
+            part = jnp.where(aux == g, y[32 * g : 32 * g + 32, 128 * n : 128 * n + 128], part)
+        y_ref[32 * n : 32 * n + 32, :] = part
+
+
+def ladder(vir_s, vir_ref, b1_ref, f_ref, t_ref, y_ref, out_ref, hi_ref, lo_ref, acc_ref):
     o, v = occ_at(), vir_at()
     acc_ref[...] = jnp.zeros_like(acc_ref)
     c_lane = jnp.broadcast_to(vir_ref[...], (128, 128))
@@ -251,27 +264,24 @@
         return carry
 
     lax.fori_loop(0, 8, step, 0, unroll=True)
-
-
-def join(p3_ref, y_ref, _, out_ref):
-    y = y_ref[0]
-    for p in range(1, 8):
-        y = y + y_ref[p]
     for a in range(8):
-        rows = jnp.transpose(p3_ref[a * 128 : a * 128 + 128, :])
+        rows = jnp.transpose(acc_ref[a * 128 : a * 128 + 128, :])
         for p in range(8):
             out_ref[p, 16 * a : 16 * a + 16, :] = rows[16 * p : 16 * p + 16, :]
     for p in range(8):
-        out_ref[p, 128:160, :] = y
-
-
-def finish(occ_s, vir_ref, r3_ref, chat_ref, out_ref, sum_ref):
+        out_ref[p, 128:320, :] = y_ref[...]
+
+
+def finish(occ_s, vir_ref, r3_ref, chat_ref, pick_ref, aux_ref, out_ref, sum_ref):
     o = occ_at()
-    total = r3_ref[0, 0:128, :]
+    total = r3_ref[0]
     for p in range(1, 8):
-        total = total + r3_ref[p, 0:128, :]
-    sum_ref[...] = total
-    z = dot_t(jnp.concatenate([r3_ref[p, 128:160, :] for p in range(8)], axis=0), chat_ref[...], lax.Precision.HIGH)
+        total = total + r3_ref[p]
+    sum_ref[...] = total[0:128]
+    y = jnp.concatenate([total[128 + 32 * n : 160 + 32 * n] for n in range(6)], axis=1)
+    aux = jnp.concatenate([aux_ref[n : n + 1, :] for n in range(6)], axis=1)
+    hi, lo = split(jnp.concatenate([jnp.where(aux == g, y, 0.0) for g in range(NG)], axis=0))
+    z = dot3(dot_t(hi, pick_ref[...]) + dot_t(lo, pick_ref[...]), chat_ref[...], dot_t)
     for j in range(4):
         label = vir_ref[...] ^ occ_s[o * 4 + j]
         part = jnp.zeros((32, 128), F32)
@@ -293,11 +303,11 @@
         (2 * 2 * 24 * 96 * 1024, 1300000), 56 * 2**20,
     )(vir, aux, row, b, t)
     r1 = swap(p1, OCC)
-    ch, sw, fits = pl.pallas_call(
+    ch, sw, pick, fits = pl.pallas_call(
         fold_ov,
-        out_shape=(shape((32, 128), F32), shape((128, 128), F32), shape((1,), jnp.int32)),
+        out_shape=(shape((32, 128), F32), shape((128, 128), F32), shape((SG, 768), BF16), shape((1,), jnp.int32)),
         in_specs=[SMEM, SMEM, VMEM, VMEM, VMEM],
-        out_specs=(VMEM, VMEM, SMEM),
+        out_specs=(VMEM, VMEM, VMEM, SMEM),
         compiler_params=pltpu.CompilerParams(vmem_limit_bytes=LIMIT),
         cost_estimate=pl.CostEstimate(flops=2 * 8 * 768 * 768, bytes_accessed=300000, transcendentals=0),
     )(vir, occ, aux, jnp.transpose(c, (1, 2, 0)), t)
@@ -307,28 +317,23 @@
     )(vir, aux, row, r1, ch, sw)
     r2 = swap(p2, ZY)
     b1 = call(
-        refold_rows, shape((SG, 1024), F32), 1, 3, [pltpu.VMEM((2048, 128), F32)], (2 * 128 * 2048 * 2048, 1700000)
+        refold_rows, shape((384, 1024), BF16), 1, 3, [pltpu.VMEM((2048, 128), F32)], (2 * 128 * 2048 * 2048, 1700000)
     )(vir, aux, row, r1)
     o2 = lax.ppermute(r2, "core", [(0, 1), (1, 0)])
     staged = shape((16, 16, 8, 128), F32)
-    yp, chat, cat, f, amps = call(
-        cycle_first, (shape((8, 32, 128), F32), shape((512, 128), F32), shape((384, 1024), BF16), staged, staged), 1, 5,
-        [pltpu.VMEM((16, 48, 128), F32)],
-        (6 * 2 * 256 * 512 * 128, 4000000),
-    )(occ, row, r2, o2, t, b1)
-    yr = swap(yp, OCC)
+    y, chat, f, amps = call(
+        cycle_first, (shape((192, 128), F32), shape((512, 128), F32), staged, staged), 1, 6,
+        [pltpu.VMEM((16, 48, 128), F32)], (6 * 2 * 256 * 512 * 128, 4000000),
+    )(occ, row, r2, o2, t, pick, aux)
     p3 = call(
-        ladder, shape((1024, 128), F32), 1, 5,
-        [
-            pltpu.VMEM((1024, 256), BF16),
-            pltpu.VMEM((1024, 256), BF16),
-        ],
+        ladder, shape((8, 320, 128), F32), 1, 5,
+        [pltpu.VMEM((1024, 256), BF16), pltpu.VMEM((1024, 256), BF16), pltpu.VMEM((1024, 128), F32)],
         (6 * 2048 * 1024 * 256, 4000000),
-    )(vir, row, cat, f, amps, chat)
-    r3 = swap(call(join, shape((8, 160, 128), F32), 0, 3, (), (0, 1300000))(p3, yr, chat), OCC)
+    )(vir, row, b1, f, amps, y)
+    r3 = swap(p3, OCC)
     out = call(
-        finish, shape((4, 4, 8, 128), F32), 1, 3, [pltpu.VMEM((128, 128), F32)], (6 * 2 * 256 * 512 * 128, 2000000)
-    )(occ, row, r3, chat)
+        finish, shape((4, 4, 8, 128), F32), 1, 5, [pltpu.VMEM((128, 128), F32)], (6 * 2 * 256 * 512 * 128, 2000000)
+    )(occ, row, r3, chat, pick, aux)
     return out, fits
 
 

time: 89.6 us -> 88.5 us (0.988)
  waiting for transfers between devices: 25.8 us -> 32.8 us
  starting transfers between devices: 19.4 us -> 13.1 us
  local copies, waits for them, and re-layouts: 2.02 us -> 0.03 us
    all_to_all x3 -> x2, waiting for transfers between devices: 25.7 us -> 32.6 us  [swap(): return lax.all_to_all(x, axes, 0, 0, tiled=True)]
    all_to_all x3 -> x2, starting transfers between devices: 17.4 us -> 11 us  [swap(): return lax.all_to_all(x, axes, 0, 0, tiled=True)]
    unnamed x14 -> x12, local copies, waits for them, and re-layouts: 2.02 us -> 0.03 us
    pallas_call x5 -> x4, Pallas kernels: 12.9 us -> 13.3 us  [the longest x1 6.84 us: folded(): call(ladder, shape((8, 320, 128), F32), 1, 5, [pltpu.VMEM((1024, 256), BF...]
  transfers between devices with their start and end apart: 4 -> 3, of which waited for: 4 -> 3; matrix products, arithmetic and copies ran while one was open for 0% -> 0% of each run, Pallas kernels for 11% -> 5%
where the time goes in v5:
time: 88.5 us; the launch traced here: 88.2 us
  waiting for transfers between devices  32.8 us (37%)
  blocking collectives  21.7 us (25%)
  Pallas kernels  19.8 us (22%)
  starting transfers between devices  13.1 us (15%)
    all_to_all x2, waiting for transfers between devices, swap(): return lax.all_to_all(x, axes, 0, 0, tiled=True)  32.6 us
    all_to_all x1, blocking collectives, swap(): return lax.all_to_all(x, axes, 0, 0, tiled=True)  21.7 us
    all_to_all x2, starting transfers between devices, swap(): return lax.all_to_all(x, axes, 0, 0, tiled=True)  11 us
    pallas_call x1, Pallas kernels, folded(): call(ladder, shape((8, 320, 128), F32), 1, 5, [pltpu.VMEM((1024, 256), BF...  6.84 us
    pallas_call x1, Pallas kernels, folded(): call(fold_local, shape((8, 8 * SL + 16, 128), F32), 1, 4, [pltpu.VMEM((8,...  2.93 us
    pallas_call x1, Pallas kernels, folded(): call(refold_rows, shape((384, 1024), BF16), 1, 3, [pltpu.VMEM((2048, 128)...  2.41 us
    pallas_call x1, Pallas kernels, folded(): call(finish, shape((4, 4, 8, 128), F32), 1, 5, [pltpu.VMEM((128, 128), F3...  2.18 us
    ppermute x1, starting transfers between devices, folded(): o2 = lax.ppermute(r2, 'core', [(0, 1), (1, 0)])  2.08 us
  transfers between devices with their start and end apart: 3, of which 3 were waited for; matrix products, arithmetic and copies ran while one was open for 0% of the time, Pallas kernels for 5%

profile of v5, /device:TPU:1, one launch (start us, length us, event | category | flops | bytes accessed | tf_op | source)
XLA Modules:
  0.0 88.2 jit_solution(1058708733279214425)
XLA Ops:
  0.0 0.0 copy-start.6
  0.0 0.0 copy-start.8
  0.0 2.9 %shard_map.67 = f32[8,208,128]{2,1,0:T(8,128)} custom-call(s32[128]{0:T(128)} %vir_s.9, s32[6,128]{1,0:T(8,128)} %bitcast.285, s32[1,128]{1,0:T(1,128)} %bitcast.291, f32[96,8,128]{2,1,0:T(8,128)} %b_ref.1, f32[4,4,8,128]{3,2,1,0:T(8,128)} %t_ref.5), custom_call_target="tpu_custom_call" | custom-call | flops 9437184 | bytes 1300000 | tf_op jit(solution)/shard_map/pallas_call | solution.py:301
  3.0 7.5 %all-to-all-start.7 = ((f32[8,208,128]{2,1,0:T(8,128)}), f32[8,208,128]{2,1,0:T(8,128)S(1)}, u32[]{:S(2)}, u32[]{:S(2)}) async-start(f32[8,208,128]{2,1,0:T(8,128)} %shard_map.67), calls=%async_computation.7 | async-start | bytes 1703936 | tf_op jit(solution)/shard_map/all_to_all | solution.py:295
  10.4 2.1 %shard_map.66 = (f32[32,128]{1,0:T(8,128)S(1)}, f32[128,128]{1,0:T(8,128)S(1)}, bf16[128,768]{1,0:T(8,128)(2,1)S(1)}, s32[1]{0:T(128)}) custom-call(s32[128]{0:T(128)} %vir_s.9, s32[32]{0:T(128)} %occ_s.5, s32[6,128]{1,0:T(8,128)} %bitcast.286, f32[4,8,768]{2,1,0:T(8,128)} %bitcast.284, f32[4,4,8,128]{3,2,1,0:T(8,128)} %t_ref.5), custom_call_target="tpu_custom_call" | custom-call | flops 9437184 | bytes 300000 | tf_op jit(solution)/shard_map/pallas_call | solution.py:306
  12.5 13.1 %all-to-all-done.7.r1_ref = f32[8,208,128]{2,1,0:T(8,128)S(1)} async-done(((f32[8,208,128]{2,1,0:T(8,128)}), f32[8,208,128]{2,1,0:T(8,128)S(1)}, u32[]{:S(2)}, u32[]{:S(2)}) %all-to-all-start.7) | async-done | bytes 852000 | tf_op jit(solution)/shard_map/all_to_all | solution.py:295
  25.6 1.6 %shard_map.69 = f32[8,304,128]{2,1,0:T(8,128)S(1)} custom-call(s32[128]{0:T(128)} %vir_s.9, s32[6,128]{1,0:T(8,128)} %bitcast.287, s32[1,128]{1,0:T(1,128)} %bitcast.292, f32[8,208,128]{2,1,0:T(8,128)S(1)} %all-to-all-done.7.r1_ref, f32[32,128]{1,0:T(8,128)S(1)} %get-tuple-element.36.ch_ref, f32[128,128]{1,0:T(8,128)S(1)} %get-tuple-element.37.sw_ref), custom_call_target="tpu_custom_call" | custom-call | flops 134217728 | bytes 2300000 | tf_op jit(solution)/shard_map/pallas_call | solution.py:314
  27.2 21.7 %all_to_all.54.r2_ref = f32[8,304,128]{2,1,0:T(8,128)S(1)} all-to-all(f32[8,304,128]{2,1,0:T(8,128)S(1)} %shard_map.69), channel_id=1, replica_groups=mesh['yh'=2,'x'=4,'z'=4,'yl'=2,'core'=2] {'z','yl'}, dimensions={0} | all-to-all | bytes 2490368 | tf_op jit(solution)/shard_map/all_to_all | solution.py:295
  48.9 2.1 %collective-permute-start = (f32[8,304,128]{2,1,0:T(8,128)S(1)}, f32[8,304,128]{2,1,0:T(8,128)S(1)}, u32[]{:S(2)}, u32[]{:S(2)}) collective-permute-start(f32[8,304,128]{2,1,0:T(8,128)S(1)} %all_to_all.54.r2_ref), channel_id=1, source_target_pairs={{0,1},{1,0},{2,3},{3,2},{4,5},{5,4},{6,7},{7,6},{8,9},{9,8},{10,11... | collective-permute-start | bytes 3735560 | tf_op jit(solution)/shard_map/ppermute | solution.py:322
  51.0 0.0 copy-done.5
  51.0 0.0 copy-done.6
  51.0 2.4 %shard_map.68.b1_ref = bf16[384,1024]{1,0:T(8,128)(2,1)S(1)} custom-call(s32[128]{0:T(128)S(1)} %copy-done.6, s32[6,128]{1,0:T(8,128)S(1)} %bitcast.288, s32[1,128]{1,0:T(1,128)S(1)} %bitcast.293, f32[8,208,128]{2,1,0:T(8,128)S(1)} %all-to-all-done.7.r1_ref), custom_call_target="tpu_custom_call" | custom-call | flops 1073741824 | bytes 1700000 | tf_op jit(solution)/shard_map/pallas_call | solution.py:319
  53.4 0.1 collective-permute-done.o2_ref
  53.5 0.0 copy-done.1
  53.5 0.0 copy-done.8
  53.5 1.8 %shard_map.70 = (f32[192,128]{1,0:T(8,128)S(1)}, f32[512,128]{1,0:T(8,128)S(1)}, f32[16,16,8,128]{3,2,1,0:T(8,128)S(1)}, f32[16,16,8,128]{3,2,1,0:T(8,128)S(1)}) custom-call(s32[32]{0:T(128)S(1)} %copy-done.8, s32[1,128]{1,0:T(1,128)S(1)} %bitcast.294, f32[8,304,128]{2,1,0:T(8,128)S(1)} %all_to_all.54.r2_ref, ...), custom_call_target="tpu_custom_call" | custom-call | flops 201326592 | bytes 4000000 | tf_op jit(solution)/shard_map/pallas_call | solution.py:324
  55.4 0.0 copy-start
  55.4 0.0 copy-start.4
  55.4 6.8 %shard_map.71 = f32[8,320,128]{2,1,0:T(8,128)} custom-call(s32[128]{0:T(128)S(1)} %copy-done.6, s32[1,128]{1,0:T(1,128)S(1)} %bitcast.295, bf16[384,1024]{1,0:T(8,128)(2,1)S(1)} %shard_map.68.b1_ref, f32[16,16,8,128]{3,2,1,0:T(8,128)S(1)} %get-tuple-element.39.f_ref, f32[16,16,8,128]{3,2,1,0:T(8,128)S(1)} %get-tuple-element.40.t_ref, ...), custom_call_target="tpu_custom_call" | custom-call | flops 3221225472 | bytes 4000000 | tf_op jit(solution)/shard_map/pallas_call | solution.py:328
  62.2 3.6 %all-to-all-start.9 = ((f32[8,320,128]{2,1,0:T(8,128)}), f32[8,320,128]{2,1,0:T(8,128)S(1)}, u32[]{:S(2)}, u32[]{:S(2)}) async-start(f32[8,320,128]{2,1,0:T(8,128)} %shard_map.71), calls=%async_computation.9 | async-start | bytes 2621440 | tf_op jit(solution)/shard_map/all_to_all | solution.py:295
  66.5 19.5 %all-to-all-done.9.r3_ref = f32[8,320,128]{2,1,0:T(8,128)S(1)} async-done(((f32[8,320,128]{2,1,0:T(8,128)}), f32[8,320,128]{2,1,0:T(8,128)S(1)}, u32[]{:S(2)}, u32[]{:S(2)}) %all-to-all-start.9) | async-done | bytes 1310752 | tf_op jit(solution)/shard_map/all_to_all | solution.py:295
  86.0 2.2 %shard_map.72 = f32[4,4,8,128]{3,2,1,0:T(8,128)} custom-call(s32[32]{0:T(128)S(1)} %copy-done.8, s32[1,128]{1,0:T(1,128)S(1)} %bitcast.296, f32[8,320,128]{2,1,0:T(8,128)S(1)} %all-to-all-done.9.r3_ref, f32[512,128]{1,0:T(8,128)S(1)} %get-tuple-element.42.chat_ref, bf16[128,768]{1,0:T(8,128)(2,1)S(1)} %get-tuple-element.38.pick_ref, s32[6,128]{1,0:T(8,128)S(1)} %bitcast.290), custom_call_target="tpu_custom_call" | custom-call | flops 201326592 | bytes 2000000 | tf_op jit(solution)/shard_map/pallas_call | solution.py:334
  88.2 0.0 copy-done
  88.2 0.0 copy-done.4
  (3 shorter events, 0.0 us)
Async XLA Ops:
  0.0 51.0 %copy-start.5 = (s32[768]{0:T(1024)S(1)}, s32[768]{0:T(1024)}, u32[]{:S(2)}) copy-start(s32[768]{0:T(1024)} %param.13) | copy-start | bytes 9220
  0.0 51.0 %copy-start.6 = (s32[128]{0:T(128)S(1)}, s32[128]{0:T(128)}, u32[]{:S(2)}) copy-start(s32[128]{0:T(128)} %vir_s.9) | copy-start | bytes 1540
  0.0 53.5 %copy-start.1 = (f32[4,4,8,128]{3,2,1,0:T(8,128)S(1)}, f32[4,4,8,128]{3,2,1,0:T(8,128)}, u32[]{:S(2)}) copy-start(f32[4,4,8,128]{3,2,1,0:T(8,128)} %t_ref.5) | copy-start | bytes 196612
  0.0 53.5 %copy-start.8 = (s32[32]{0:T(128)S(1)}, s32[32]{0:T(128)}, u32[]{:S(2)}) copy-start(s32[32]{0:T(128)} %occ_s.5) | copy-start | bytes 388
  3.0 22.7 %all-to-all-start.7 = ((f32[8,208,128]{2,1,0:T(8,128)}), f32[8,208,128]{2,1,0:T(8,128)S(1)}, u32[]{:S(2)}, u32[]{:S(2)}) async-start(f32[8,208,128]{2,1,0:T(8,128)} %shard_map.67), calls=%async_computation.7 | async-start | bytes 1703936 | tf_op jit(solution)/shard_map/all_to_all | solution.py:295
  48.9 4.6 %collective-permute-start = (f32[8,304,128]{2,1,0:T(8,128)S(1)}, f32[8,304,128]{2,1,0:T(8,128)S(1)}, u32[]{:S(2)}, u32[]{:S(2)}) collective-permute-start(f32[8,304,128]{2,1,0:T(8,128)S(1)} %all_to_all.54.r2_ref), channel_id=1, source_target_pairs={{0,1},{1,0},{2,3},{3,2},{4,5},{5,4},{6,7},{7,6},{8,9},{9,8},{10,11... | collective-permute-start | bytes 3735560 | tf_op jit(solution)/shard_map/ppermute | solution.py:322
  55.4 32.8 %copy-start = (f32[96,8,128]{2,1,0:T(8,128)S(1)}, f32[96,8,128]{2,1,0:T(8,128)}, u32[]{:S(2)}) copy-start(f32[96,8,128]{2,1,0:T(8,128)} %b_ref.1) | copy-start | bytes 1179652
  55.4 32.8 %copy-start.4 = (f32[768,4,8]{0,2,1:T(8,128)S(1)}, f32[768,4,8]{0,2,1:T(8,128)}, u32[]{:S(2)}) copy-start(f32[768,4,8]{0,2,1:T(8,128)} %param.10) | copy-start | bytes 294916
  62.2 23.7 %all-to-all-start.9 = ((f32[8,320,128]{2,1,0:T(8,128)}), f32[8,320,128]{2,1,0:T(8,128)S(1)}, u32[]{:S(2)}, u32[]{:S(2)}) async-start(f32[8,320,128]{2,1,0:T(8,128)} %shard_map.71), calls=%async_computation.9 | async-start | bytes 2621440 | tf_op jit(solution)/shard_map/all_to_all | solution.py:295

commit v6 on v5

--- a/solution.py
+++ b/solution.py
@@ -272,23 +272,37 @@
         out_ref[p, 128:320, :] = y_ref[...]
 
 
-def finish(occ_s, vir_ref, r3_ref, chat_ref, pick_ref, aux_ref, out_ref, sum_ref):
+def cycle_and_ladder(
+    vir_s, occ_s, vir_ref, aux_ref, r2_ref, o2_ref, t_ref, pick_ref, b1_ref, out_ref, chat_ref,
+    y_ref, f_ref, amps_ref, got_ref, hi_ref, lo_ref, acc_ref,
+):
+    cycle_first(occ_s, vir_ref, r2_ref, o2_ref, t_ref, pick_ref, aux_ref, y_ref, chat_ref, f_ref, amps_ref, got_ref)
+    ladder(vir_s, vir_ref, b1_ref, f_ref, amps_ref, y_ref, out_ref, hi_ref, lo_ref, acc_ref)
+
+
+def unfold(occ_s, vir_ref, chat_ref, pick_ref, aux_ref, hi_ref, lo_ref):
     o = occ_at()
+    aux = jnp.concatenate([aux_ref[n : n + 1, :] for n in range(6)], axis=1)
+    label = jnp.transpose(jnp.broadcast_to(vir_ref[...], (128, 128)))[:, :1]
+    for j in range(4):
+        hi, lo = split(chat_ref[128 * j : 128 * j + 128, :])
+        wide = dot(hi, pick_ref[...]) + dot(lo, pick_ref[...])
+        hi, lo = split(jnp.where((label ^ occ_s[o * 4 + j]) == aux, wide, 0.0))
+        hi_ref[128 * j : 128 * j + 128, :] = hi
+        lo_ref[128 * j : 128 * j + 128, :] = lo
+
+
+def finish(r3_ref, ch_ref, cl_ref, out_ref, sum_ref):
     total = r3_ref[0]
     for p in range(1, 8):
         total = total + r3_ref[p]
     sum_ref[...] = total[0:128]
-    y = jnp.concatenate([total[128 + 32 * n : 160 + 32 * n] for n in range(6)], axis=1)
-    aux = jnp.concatenate([aux_ref[n : n + 1, :] for n in range(6)], axis=1)
-    hi, lo = split(jnp.concatenate([jnp.where(aux == g, y, 0.0) for g in range(NG)], axis=0))
-    z = dot3(dot_t(hi, pick_ref[...]) + dot_t(lo, pick_ref[...]), chat_ref[...], dot_t)
-    for j in range(4):
-        label = vir_ref[...] ^ occ_s[o * 4 + j]
-        part = jnp.zeros((32, 128), F32)
-        for g in range(NG):
-            part = jnp.where(label == g, z[g * 32 : g * 32 + 32, j * 128 : j * 128 + 128], part)
-        for i in range(4):
-            out_ref[i, j] = sum_ref[pl.ds(i * 4 + j, 8, stride=16), :] + part[8 * i : 8 * i + 8, :]
+    hi, lo = split(jnp.concatenate([total[128 + 32 * n : 160 + 32 * n] for n in range(6)], axis=1))
+    z = dot_t(hi, ch_ref[...]) + dot_t(hi, cl_ref[...]) + dot_t(lo, ch_ref[...])
+    for i in range(4):
+        for j in range(4):
+            part = z[8 * i : 8 * i + 8, 128 * j : 128 * j + 128]
+            out_ref[i, j] = sum_ref[pl.ds(i * 4 + j, 8, stride=16), :] + part
 
 
 def swap(x, axes):
@@ -320,20 +334,27 @@
         refold_rows, shape((384, 1024), BF16), 1, 3, [pltpu.VMEM((2048, 128), F32)], (2 * 128 * 2048 * 2048, 1700000)
     )(vir, aux, row, r1)
     o2 = lax.ppermute(r2, "core", [(0, 1), (1, 0)])
-    staged = shape((16, 16, 8, 128), F32)
-    y, chat, f, amps = call(
-        cycle_first, (shape((192, 128), F32), shape((512, 128), F32), staged, staged), 1, 6,
-        [pltpu.VMEM((16, 48, 128), F32)], (6 * 2 * 256 * 512 * 128, 4000000),
-    )(occ, row, r2, o2, t, pick, aux)
-    p3 = call(
-        ladder, shape((8, 320, 128), F32), 1, 5,
-        [pltpu.VMEM((1024, 256), BF16), pltpu.VMEM((1024, 256), BF16), pltpu.VMEM((1024, 128), F32)],
-        (6 * 2048 * 1024 * 256, 4000000),
-    )(vir, row, b1, f, amps, y)
+    staged = (16, 16, 8, 128)
+    p3, chat = call(
+        cycle_and_ladder, (shape((8, 320, 128), F32), shape((512, 128), F32)), 2, 7,
+        [
+            pltpu.VMEM((192, 128), F32),
+            pltpu.VMEM(staged, F32),
+            pltpu.VMEM(staged, F32),
+            pltpu.VMEM((16, 48, 128), F32),
+            pltpu.VMEM((1024, 256), BF16),
+            pltpu.VMEM((1024, 256), BF16),
+            pltpu.VMEM((1024, 128), F32),
+        ],
+        (6 * 2048 * 1024 * 256 + 6 * 2 * 256 * 512 * 128, 5000000),
+    )(vir, occ, row, aux, r2, o2, t, pick, b1)
     r3 = swap(p3, OCC)
+    ch, cl = call(
+        unfold, (shape((512, 768), BF16), shape((512, 768), BF16)), 1, 4, (), (4 * 512 * 768 * 128, 2000000)
+    )(occ, row, chat, pick, aux)
     out = call(
-        finish, shape((4, 4, 8, 128), F32), 1, 5, [pltpu.VMEM((128, 128), F32)], (6 * 2 * 256 * 512 * 128, 2000000)
-    )(occ, row, r3, chat, pick, aux)
+        finish, shape((4, 4, 8, 128), F32), 0, 3, [pltpu.VMEM((128, 128), F32)], (6 * 32 * 512 * 768, 3000000)
+    )(r3, ch, cl)
     return out, fits
 
 

time: 88.5 us -> 86.9 us (0.982)
  waiting for transfers between devices: 32.8 us -> 31.7 us
    all_to_all x2, waiting for transfers between devices: 32.6 us -> 31.5 us  [swap(): return lax.all_to_all(x, axes, 0, 0, tiled=True)]
  transfers between devices with their start and end apart: 3 -> 3, of which waited for: 3 -> 3; matrix products, arithmetic and copies ran while one was open for 0% -> 0% of each run, Pallas kernels for 5% -> 6%
where the time goes in v6:
time: 86.9 us; the launch traced here: 86.6 us
  waiting for transfers between devices  31.7 us (36%)
  blocking collectives  21.7 us (25%)
  Pallas kernels  19.4 us (22%)
  starting transfers between devices  13.1 us (15%)
    all_to_all x2, waiting for transfers between devices, swap(): return lax.all_to_all(x, axes, 0, 0, tiled=True)  31.5 us
    all_to_all x1, blocking collectives, swap(): return lax.all_to_all(x, axes, 0, 0, tiled=True)  21.7 us
    all_to_all x2, starting transfers between devices, swap(): return lax.all_to_all(x, axes, 0, 0, tiled=True)  11 us
    pallas_call x1, Pallas kernels, folded(): call(cycle_and_ladder, (shape((8, 320, 128), F32), shape((512, 128), F32)...  7.92 us
    pallas_call x1, Pallas kernels, folded(): call(fold_local, shape((8, 8 * SL + 16, 128), F32), 1, 4, [pltpu.VMEM((8,...  2.92 us
    pallas_call x1, Pallas kernels, folded(): call(refold_rows, shape((384, 1024), BF16), 1, 3, [pltpu.VMEM((2048, 128)...  2.41 us
    ppermute x1, starting transfers between devices, folded(): o2 = lax.ppermute(r2, 'core', [(0, 1), (1, 0)])  2.08 us
    pallas_call x1, Pallas kernels, folded(): pl.pallas_call(fold_ov, out_shape=(shape((32, 128), F32), shape((128, 128...  2.06 us
  transfers between devices with their start and end apart: 3, of which 3 were waited for; matrix products, arithmetic and copies ran while one was open for 0% of the time, Pallas kernels for 6%

profile of v6, /device:TPU:1, one launch (start us, length us, event | category | flops | bytes accessed | tf_op | source)
XLA Modules:
  0.0 86.6 jit_solution(13901955386328941169)
XLA Ops:
  0.0 0.0 copy-start.3
  0.0 0.0 copy-start.4
  0.0 0.0 copy-start.1
  0.0 0.0 copy-start.6
  0.0 2.9 %shard_map.67 = f32[8,208,128]{2,1,0:T(8,128)} custom-call(s32[128]{0:T(128)} %vir_s.9, s32[6,128]{1,0:T(8,128)} %bitcast.285, s32[1,128]{1,0:T(1,128)} %bitcast.291, f32[96,8,128]{2,1,0:T(8,128)} %b_ref.1, f32[4,4,8,128]{3,2,1,0:T(8,128)} %t_ref.5), custom_call_target="tpu_custom_call" | custom-call | flops 9437184 | bytes 1300000 | tf_op jit(solution)/shard_map/pallas_call | solution.py:315
  2.9 7.5 %all-to-all-start.7 = ((f32[8,208,128]{2,1,0:T(8,128)}), f32[8,208,128]{2,1,0:T(8,128)S(1)}, u32[]{:S(2)}, u32[]{:S(2)}) async-start(f32[8,208,128]{2,1,0:T(8,128)} %shard_map.67), calls=%async_computation.7 | async-start | bytes 1703936 | tf_op jit(solution)/shard_map/all_to_all | solution.py:309
  10.4 2.1 %shard_map.66 = (f32[32,128]{1,0:T(8,128)S(1)}, f32[128,128]{1,0:T(8,128)S(1)}, bf16[128,768]{1,0:T(8,128)(2,1)S(1)}, s32[1]{0:T(128)}) custom-call(s32[128]{0:T(128)} %vir_s.9, s32[32]{0:T(128)} %occ_s.5, s32[6,128]{1,0:T(8,128)} %bitcast.286, f32[4,8,768]{2,1,0:T(8,128)} %bitcast.284, f32[4,4,8,128]{3,2,1,0:T(8,128)} %t_ref.5), custom_call_target="tpu_custom_call" | custom-call | flops 9437184 | bytes 300000 | tf_op jit(solution)/shard_map/pallas_call | solution.py:320
  12.5 13.1 %all-to-all-done.7.r1_ref = f32[8,208,128]{2,1,0:T(8,128)S(1)} async-done(((f32[8,208,128]{2,1,0:T(8,128)}), f32[8,208,128]{2,1,0:T(8,128)S(1)}, u32[]{:S(2)}, u32[]{:S(2)}) %all-to-all-start.7) | async-done | bytes 852000 | tf_op jit(solution)/shard_map/all_to_all | solution.py:309
  25.6 1.6 %shard_map.68 = f32[8,304,128]{2,1,0:T(8,128)S(1)} custom-call(s32[128]{0:T(128)} %vir_s.9, s32[6,128]{1,0:T(8,128)} %bitcast.287, s32[1,128]{1,0:T(1,128)} %bitcast.292, f32[8,208,128]{2,1,0:T(8,128)S(1)} %all-to-all-done.7.r1_ref, f32[32,128]{1,0:T(8,128)S(1)} %get-tuple-element.36.ch_ref, f32[128,128]{1,0:T(8,128)S(1)} %get-tuple-element.37.sw_ref), custom_call_target="tpu_custom_call" | custom-call | flops 134217728 | bytes 2300000 | tf_op jit(solution)/shard_map/pallas_call | solution.py:328
  27.2 21.7 %all_to_all.54.r2_ref = f32[8,304,128]{2,1,0:T(8,128)S(1)} all-to-all(f32[8,304,128]{2,1,0:T(8,128)S(1)} %shard_map.68), channel_id=1, replica_groups=mesh['yh'=2,'x'=4,'z'=4,'yl'=2,'core'=2] {'z','yl'}, dimensions={0} | all-to-all | bytes 2490368 | tf_op jit(solution)/shard_map/all_to_all | solution.py:309
  48.9 2.1 %collective-permute-start = (f32[8,304,128]{2,1,0:T(8,128)S(1)}, f32[8,304,128]{2,1,0:T(8,128)S(1)}, u32[]{:S(2)}, u32[]{:S(2)}) collective-permute-start(f32[8,304,128]{2,1,0:T(8,128)S(1)} %all_to_all.54.r2_ref), channel_id=1, source_target_pairs={{0,1},{1,0},{2,3},{3,2},{4,5},{5,4},{6,7},{7,6},{8,9},{9,8},{10,11... | collective-permute-start | bytes 3735560 | tf_op jit(solution)/shard_map/ppermute | solution.py:336
  50.9 0.0 copy-done.3
  50.9 0.0 copy-done.4
  51.0 2.4 %shard_map.69.b1_ref = bf16[384,1024]{1,0:T(8,128)(2,1)S(1)} custom-call(s32[128]{0:T(128)S(1)} %copy-done.4, s32[6,128]{1,0:T(8,128)S(1)} %bitcast.288, s32[1,128]{1,0:T(1,128)S(1)} %bitcast.293, f32[8,208,128]{2,1,0:T(8,128)S(1)} %all-to-all-done.7.r1_ref), custom_call_target="tpu_custom_call" | custom-call | flops 1073741824 | bytes 1700000 | tf_op jit(solution)/shard_map/pallas_call | solution.py:333
  53.4 0.1 collective-permute-done.o2_ref
  53.5 0.0 copy-done.1
  53.5 0.0 copy-done.6
  53.5 7.9 %shard_map.70 = (f32[8,320,128]{2,1,0:T(8,128)}, f32[512,128]{1,0:T(8,128)S(1)}) custom-call(s32[128]{0:T(128)S(1)} %copy-done.4, s32[32]{0:T(128)S(1)} %copy-done.6, s32[1,128]{1,0:T(1,128)S(1)} %bitcast.294, s32[6,128]{1,0:T(8,128)S(1)} %bitcast.289, f32[8,304,128]{2,1,0:T(8,128)S(1)} %all_to_all.54.r2_ref, ...), custom_call_target="tpu_custom_call" | custom-call | flops 3422552064 | bytes 5000000 | tf_op jit(solution)/shard_map/pallas_call | solution.py:338
  61.4 3.6 %all-to-all-start.9 = ((f32[8,320,128]{2,1,0:T(8,128)}), f32[8,320,128]{2,1,0:T(8,128)S(1)}, u32[]{:S(2)}, u32[]{:S(2)}) async-start(f32[8,320,128]{2,1,0:T(8,128)} %get-tuple-element.39), calls=%async_computation.9 | async-start | bytes 2621440 | tf_op jit(solution)/shard_map/all_to_all | solution.py:309
  65.7 1.1 %shard_map.71 = (bf16[512,768]{1,0:T(8,128)(2,1)S(1)}, bf16[512,768]{1,0:T(8,128)(2,1)S(1)}) custom-call(s32[32]{0:T(128)S(1)} %copy-done.6, s32[1,128]{1,0:T(1,128)S(1)} %bitcast.295, f32[512,128]{1,0:T(8,128)S(1)} %get-tuple-element.40.chat_ref, bf16[128,768]{1,0:T(8,128)(2,1)S(1)} %get-tuple-element.38.pick_ref, s32[6,128]{1,0:T(8,128)S(1)} %bitcast.290), custom_call_target="tpu_custom_call" | custom-call | flops 201326592 | bytes 2000000 | tf_op jit(solution)/shard_map/pallas_call | solution.py:352
  66.8 18.4 %all-to-all-done.9.r3_ref = f32[8,320,128]{2,1,0:T(8,128)S(1)} async-done(((f32[8,320,128]{2,1,0:T(8,128)}), f32[8,320,128]{2,1,0:T(8,128)S(1)}, u32[]{:S(2)}, u32[]{:S(2)}) %all-to-all-start.9) | async-done | bytes 1310752 | tf_op jit(solution)/shard_map/all_to_all | solution.py:309
  85.2 1.4 %shard_map.72 = f32[4,4,8,128]{3,2,1,0:T(8,128)} custom-call(f32[8,320,128]{2,1,0:T(8,128)S(1)} %all-to-all-done.9.r3_ref, bf16[512,768]{1,0:T(8,128)(2,1)S(1)} %get-tuple-element.41.ch_ref, bf16[512,768]{1,0:T(8,128)(2,1)S(1)} %get-tuple-element.42.cl_ref), custom_call_target="tpu_custom_call" | custom-call | flops 75497472 | bytes 3000000 | tf_op jit(solution)/shard_map/pallas_call | solution.py:355
  (1 shorter events, 0.0 us)
Async XLA Ops:
  0.0 50.9 %copy-start.3 = (s32[768]{0:T(1024)S(1)}, s32[768]{0:T(1024)}, u32[]{:S(2)}) copy-start(s32[768]{0:T(1024)} %param.13) | copy-start | bytes 9220
  0.0 50.9 %copy-start.4 = (s32[128]{0:T(128)S(1)}, s32[128]{0:T(128)}, u32[]{:S(2)}) copy-start(s32[128]{0:T(128)} %vir_s.9) | copy-start | bytes 1540
  0.0 53.5 %copy-start.1 = (f32[4,4,8,128]{3,2,1,0:T(8,128)S(1)}, f32[4,4,8,128]{3,2,1,0:T(8,128)}, u32[]{:S(2)}) copy-start(f32[4,4,8,128]{3,2,1,0:T(8,128)} %t_ref.5) | copy-start | bytes 196612
  0.0 53.5 %copy-start.6 = (s32[32]{0:T(128)S(1)}, s32[32]{0:T(128)}, u32[]{:S(2)}) copy-start(s32[32]{0:T(128)} %occ_s.5) | copy-start | bytes 388
  2.9 22.7 %all-to-all-start.7 = ((f32[8,208,128]{2,1,0:T(8,128)}), f32[8,208,128]{2,1,0:T(8,128)S(1)}, u32[]{:S(2)}, u32[]{:S(2)}) async-start(f32[8,208,128]{2,1,0:T(8,128)} %shard_map.67), calls=%async_computation.7 | async-start | bytes 1703936 | tf_op jit(solution)/shard_map/all_to_all | solution.py:309
  48.9 4.6 %collective-permute-start = (f32[8,304,128]{2,1,0:T(8,128)S(1)}, f32[8,304,128]{2,1,0:T(8,128)S(1)}, u32[]{:S(2)}, u32[]{:S(2)}) collective-permute-start(f32[8,304,128]{2,1,0:T(8,128)S(1)} %all_to_all.54.r2_ref), channel_id=1, source_target_pairs={{0,1},{1,0},{2,3},{3,2},{4,5},{5,4},{6,7},{7,6},{8,9},{9,8},{10,11... | collective-permute-start | bytes 3735560 | tf_op jit(solution)/shard_map/ppermute | solution.py:336
  61.4 23.7 %all-to-all-start.9 = ((f32[8,320,128]{2,1,0:T(8,128)}), f32[8,320,128]{2,1,0:T(8,128)S(1)}, u32[]{:S(2)}, u32[]{:S(2)}) async-start(f32[8,320,128]{2,1,0:T(8,128)} %get-tuple-element.39), calls=%async_computation.9 | async-start | bytes 2621440 | tf_op jit(solution)/shard_map/all_to_all | solution.py:309

commit v7 on v6

--- a/solution.py
+++ b/solution.py
@@ -91,7 +91,8 @@
     for x in range(8):
         keep = (y_row ^ vir_s[v * 8 + x]) == q_sub[:96]
         hi, lo = split(jnp.where(keep, b_ref[:, x, :], 0.0))
-        folded = dot(pick, hi) + dot(pick, lo)
+        both = dot(pick, jnp.concatenate([hi, lo], axis=1))
+        folded = both[:, :128] + both[:, 128:]
         for peer in range(8):
             out_ref[peer, x * SL : (x + 1) * SL, :] = folded
     amps = t_ref[...].reshape(16, 8, 128)

time: 86.9 us -> 86.9 us (level)
  no operation moved by 1% of the time
where the time goes in v7:
time: 86.9 us; the launch traced here: 86.6 us
  waiting for transfers between devices  31.7 us (36%)
  blocking collectives  21.7 us (25%)
  Pallas kernels  19.4 us (22%)
  starting transfers between devices  13.1 us (15%)
    all_to_all x2, waiting for transfers between devices, swap(): return lax.all_to_all(x, axes, 0, 0, tiled=True)  31.5 us
    all_to_all x1, blocking collectives, swap(): return lax.all_to_all(x, axes, 0, 0, tiled=True)  21.7 us
    all_to_all x2, starting transfers between devices, swap(): return lax.all_to_all(x, axes, 0, 0, tiled=True)  11 us
    pallas_call x1, Pallas kernels, folded(): call(cycle_and_ladder, (shape((8, 320, 128), F32), shape((512, 128), F32)...  7.92 us
    pallas_call x1, Pallas kernels, folded(): call(fold_local, shape((8, 8 * SL + 16, 128), F32), 1, 4, [pltpu.VMEM((8,...  2.92 us
    pallas_call x1, Pallas kernels, folded(): call(refold_rows, shape((384, 1024), BF16), 1, 3, [pltpu.VMEM((2048, 128)...  2.41 us
    ppermute x1, starting transfers between devices, folded(): o2 = lax.ppermute(r2, 'core', [(0, 1), (1, 0)])  2.08 us
    pallas_call x1, Pallas kernels, folded(): pl.pallas_call(fold_ov, out_shape=(shape((32, 128), F32), shape((128, 128...  2.06 us
  transfers between devices with their start and end apart: 3, of which 3 were waited for; matrix products, arithmetic and copies ran while one was open for 0% of the time, Pallas kernels for 6%

profile of v7, /device:TPU:1, one launch (start us, length us, event | category | flops | bytes accessed | tf_op | source)
XLA Modules:
  0.0 86.6 jit_solution(631857098406278305)
XLA Ops:
  0.0 0.0 copy-start.3
  0.0 0.0 copy-start.4
  0.0 0.0 copy-start.1
  0.0 0.0 copy-start.6
  0.0 2.9 %shard_map.67 = f32[8,208,128]{2,1,0:T(8,128)} custom-call(s32[128]{0:T(128)} %vir_s.9, s32[6,128]{1,0:T(8,128)} %bitcast.285, s32[1,128]{1,0:T(1,128)} %bitcast.291, f32[96,8,128]{2,1,0:T(8,128)} %b_ref.1, f32[4,4,8,128]{3,2,1,0:T(8,128)} %t_ref.5), custom_call_target="tpu_custom_call" | custom-call | flops 9437184 | bytes 1300000 | tf_op jit(solution)/shard_map/pallas_call | solution.py:316
  2.9 7.5 %all-to-all-start.7 = ((f32[8,208,128]{2,1,0:T(8,128)}), f32[8,208,128]{2,1,0:T(8,128)S(1)}, u32[]{:S(2)}, u32[]{:S(2)}) async-start(f32[8,208,128]{2,1,0:T(8,128)} %shard_map.67), calls=%async_computation.7 | async-start | bytes 1703936 | tf_op jit(solution)/shard_map/all_to_all | solution.py:310
  10.4 2.1 %shard_map.66 = (f32[32,128]{1,0:T(8,128)S(1)}, f32[128,128]{1,0:T(8,128)S(1)}, bf16[128,768]{1,0:T(8,128)(2,1)S(1)}, s32[1]{0:T(128)}) custom-call(s32[128]{0:T(128)} %vir_s.9, s32[32]{0:T(128)} %occ_s.5, s32[6,128]{1,0:T(8,128)} %bitcast.286, f32[4,8,768]{2,1,0:T(8,128)} %bitcast.284, f32[4,4,8,128]{3,2,1,0:T(8,128)} %t_ref.5), custom_call_target="tpu_custom_call" | custom-call | flops 9437184 | bytes 300000 | tf_op jit(solution)/shard_map/pallas_call | solution.py:321
  12.5 13.1 %all-to-all-done.7.r1_ref = f32[8,208,128]{2,1,0:T(8,128)S(1)} async-done(((f32[8,208,128]{2,1,0:T(8,128)}), f32[8,208,128]{2,1,0:T(8,128)S(1)}, u32[]{:S(2)}, u32[]{:S(2)}) %all-to-all-start.7) | async-done | bytes 852000 | tf_op jit(solution)/shard_map/all_to_all | solution.py:310
  25.6 1.6 %shard_map.68 = f32[8,304,128]{2,1,0:T(8,128)S(1)} custom-call(s32[128]{0:T(128)} %vir_s.9, s32[6,128]{1,0:T(8,128)} %bitcast.287, s32[1,128]{1,0:T(1,128)} %bitcast.292, f32[8,208,128]{2,1,0:T(8,128)S(1)} %all-to-all-done.7.r1_ref, f32[32,128]{1,0:T(8,128)S(1)} %get-tuple-element.36.ch_ref, f32[128,128]{1,0:T(8,128)S(1)} %get-tuple-element.37.sw_ref), custom_call_target="tpu_custom_call" | custom-call | flops 134217728 | bytes 2300000 | tf_op jit(solution)/shard_map/pallas_call | solution.py:329
  27.2 21.7 %all_to_all.54.r2_ref = f32[8,304,128]{2,1,0:T(8,128)S(1)} all-to-all(f32[8,304,128]{2,1,0:T(8,128)S(1)} %shard_map.68), channel_id=1, replica_groups=mesh['yh'=2,'x'=4,'z'=4,'yl'=2,'core'=2] {'z','yl'}, dimensions={0} | all-to-all | bytes 2490368 | tf_op jit(solution)/shard_map/all_to_all | solution.py:310
  48.9 2.1 %collective-permute-start = (f32[8,304,128]{2,1,0:T(8,128)S(1)}, f32[8,304,128]{2,1,0:T(8,128)S(1)}, u32[]{:S(2)}, u32[]{:S(2)}) collective-permute-start(f32[8,304,128]{2,1,0:T(8,128)S(1)} %all_to_all.54.r2_ref), channel_id=1, source_target_pairs={{0,1},{1,0},{2,3},{3,2},{4,5},{5,4},{6,7},{7,6},{8,9},{9,8},{10,11... | collective-permute-start | bytes 3735560 | tf_op jit(solution)/shard_map/ppermute | solution.py:337
  50.9 0.0 copy-done.3
  50.9 0.0 copy-done.4
  51.0 2.4 %shard_map.69.b1_ref = bf16[384,1024]{1,0:T(8,128)(2,1)S(1)} custom-call(s32[128]{0:T(128)S(1)} %copy-done.4, s32[6,128]{1,0:T(8,128)S(1)} %bitcast.288, s32[1,128]{1,0:T(1,128)S(1)} %bitcast.293, f32[8,208,128]{2,1,0:T(8,128)S(1)} %all-to-all-done.7.r1_ref), custom_call_target="tpu_custom_call" | custom-call | flops 1073741824 | bytes 1700000 | tf_op jit(solution)/shard_map/pallas_call | solution.py:334
  53.4 0.1 collective-permute-done.o2_ref
  53.5 0.0 copy-done.1
  53.5 0.0 copy-done.6
  53.5 7.9 %shard_map.70 = (f32[8,320,128]{2,1,0:T(8,128)}, f32[512,128]{1,0:T(8,128)S(1)}) custom-call(s32[128]{0:T(128)S(1)} %copy-done.4, s32[32]{0:T(128)S(1)} %copy-done.6, s32[1,128]{1,0:T(1,128)S(1)} %bitcast.294, s32[6,128]{1,0:T(8,128)S(1)} %bitcast.289, f32[8,304,128]{2,1,0:T(8,128)S(1)} %all_to_all.54.r2_ref, ...), custom_call_target="tpu_custom_call" | custom-call | flops 3422552064 | bytes 5000000 | tf_op jit(solution)/shard_map/pallas_call | solution.py:339
  61.4 3.6 %all-to-all-start.9 = ((f32[8,320,128]{2,1,0:T(8,128)}), f32[8,320,128]{2,1,0:T(8,128)S(1)}, u32[]{:S(2)}, u32[]{:S(2)}) async-start(f32[8,320,128]{2,1,0:T(8,128)} %get-tuple-element.39), calls=%async_computation.9 | async-start | bytes 2621440 | tf_op jit(solution)/shard_map/all_to_all | solution.py:310
  65.7 1.1 %shard_map.71 = (bf16[512,768]{1,0:T(8,128)(2,1)S(1)}, bf16[512,768]{1,0:T(8,128)(2,1)S(1)}) custom-call(s32[32]{0:T(128)S(1)} %copy-done.6, s32[1,128]{1,0:T(1,128)S(1)} %bitcast.295, f32[512,128]{1,0:T(8,128)S(1)} %get-tuple-element.40.chat_ref, bf16[128,768]{1,0:T(8,128)(2,1)S(1)} %get-tuple-element.38.pick_ref, s32[6,128]{1,0:T(8,128)S(1)} %bitcast.290), custom_call_target="tpu_custom_call" | custom-call | flops 201326592 | bytes 2000000 | tf_op jit(solution)/shard_map/pallas_call | solution.py:353
  66.8 18.4 %all-to-all-done.9.r3_ref = f32[8,320,128]{2,1,0:T(8,128)S(1)} async-done(((f32[8,320,128]{2,1,0:T(8,128)}), f32[8,320,128]{2,1,0:T(8,128)S(1)}, u32[]{:S(2)}, u32[]{:S(2)}) %all-to-all-start.9) | async-done | bytes 1310752 | tf_op jit(solution)/shard_map/all_to_all | solution.py:310
  85.2 1.4 %shard_map.72 = f32[4,4,8,128]{3,2,1,0:T(8,128)} custom-call(f32[8,320,128]{2,1,0:T(8,128)S(1)} %all-to-all-done.9.r3_ref, bf16[512,768]{1,0:T(8,128)(2,1)S(1)} %get-tuple-element.41.ch_ref, bf16[512,768]{1,0:T(8,128)(2,1)S(1)} %get-tuple-element.42.cl_ref), custom_call_target="tpu_custom_call" | custom-call | flops 75497472 | bytes 3000000 | tf_op jit(solution)/shard_map/pallas_call | solution.py:356
  (1 shorter events, 0.0 us)
Async XLA Ops:
  0.0 50.9 %copy-start.3 = (s32[768]{0:T(1024)S(1)}, s32[768]{0:T(1024)}, u32[]{:S(2)}) copy-start(s32[768]{0:T(1024)} %param.13) | copy-start | bytes 9220
  0.0 50.9 %copy-start.4 = (s32[128]{0:T(128)S(1)}, s32[128]{0:T(128)}, u32[]{:S(2)}) copy-start(s32[128]{0:T(128)} %vir_s.9) | copy-start | bytes 1540
  0.0 53.5 %copy-start.1 = (f32[4,4,8,128]{3,2,1,0:T(8,128)S(1)}, f32[4,4,8,128]{3,2,1,0:T(8,128)}, u32[]{:S(2)}) copy-start(f32[4,4,8,128]{3,2,1,0:T(8,128)} %t_ref.5) | copy-start | bytes 196612
  0.0 53.5 %copy-start.6 = (s32[32]{0:T(128)S(1)}, s32[32]{0:T(128)}, u32[]{:S(2)}) copy-start(s32[32]{0:T(128)} %occ_s.5) | copy-start | bytes 388
  2.9 22.7 %all-to-all-start.7 = ((f32[8,208,128]{2,1,0:T(8,128)}), f32[8,208,128]{2,1,0:T(8,128)S(1)}, u32[]{:S(2)}, u32[]{:S(2)}) async-start(f32[8,208,128]{2,1,0:T(8,128)} %shard_map.67), calls=%async_computation.7 | async-start | bytes 1703936 | tf_op jit(solution)/shard_map/all_to_all | solution.py:310
  48.9 4.6 %collective-permute-start = (f32[8,304,128]{2,1,0:T(8,128)S(1)}, f32[8,304,128]{2,1,0:T(8,128)S(1)}, u32[]{:S(2)}, u32[]{:S(2)}) collective-permute-start(f32[8,304,128]{2,1,0:T(8,128)S(1)} %all_to_all.54.r2_ref), channel_id=1, source_target_pairs={{0,1},{1,0},{2,3},{3,2},{4,5},{5,4},{6,7},{7,6},{8,9},{9,8},{10,11... | collective-permute-start | bytes 3735560 | tf_op jit(solution)/shard_map/ppermute | solution.py:337
  61.4 23.7 %all-to-all-start.9 = ((f32[8,320,128]{2,1,0:T(8,128)}), f32[8,320,128]{2,1,0:T(8,128)S(1)}, u32[]{:S(2)}, u32[]{:S(2)}) async-start(f32[8,320,128]{2,1,0:T(8,128)} %get-tuple-element.39), calls=%async_computation.9 | async-start | bytes 2621440 | tf_op jit(solution)/shard_map/all_to_all | solution.py:310
